TPU v7x, 256 devices: a whole 4x4x8 slice. The times are simulated.
256 devices in a mesh: segment: 2 (over x_lo), blk: 32 (over z, x_hi, core), mp: 4 (over y).
Axes of the slice: x: 4 (x_hi: 2, x_lo: 2; x = x_hi * 2 + x_lo), y: 4, z: 8, core: 2. Of those that a mesh axis runs over, the one named last changes fastest.
Arguments:
- segment_in: bfloat16 [2, 8192, 4096], P('segment', 'blk'), may hold values from -7.5 to 7.5
- norm_gains: float32 [2, 4096], P('segment'), may hold values from 0.25 to 1.75
- projections: bfloat16 [2, 4096, 2, 2048], P('segment', None, None, 'mp'), may hold values from -2 to 2
- live_counts: int32 [2, 32], P(None, 'blk'), may hold values from 1 to 256, 6144 in all within a row
- cotangent: bfloat16 [8192, 4096], P('blk', 'mp'), may hold values from -6 to 6
Outputs:
- segment_out: bfloat16 [2, 8192, 4096], P('segment', 'blk', 'mp')
- state_grads: bfloat16 [2, 8192, 4096], P('segment', 'blk', 'mp')
Inputs may be any that keep to these rules, and one draw needn't show every extreme that they name: `live_counts`: each row sums to 6144; every entry is at least 1; each row has an entry equal to 256.
All inputs are finite; a program needn't handle non-finite values. No bound on the sum of `live_counts` on one device may be relied on, other than what follows from the above.
Results may differ from a plain program's by a relative error of at most 0.015.
Values may be sent and summed in bfloat16 or wider, within the bound.
A program may use at most 128 MiB of HBM per device.

v0:
```python
import jax
import jax.numpy as jnp
from jax import lax
from jax.sharding import PartitionSpec as P

DH = 64
WIN = 4


EPSILON = 1e-06
SCALE = 0.125
NEGATIVE = -1e30


def from_behind(x, axis, by):
    size = lax.axis_size(axis)
    pairs = [(i, i + by) for i in range(size) if 0 <= i + by < size]
    return lax.ppermute(x, axis, pairs)


def normalize(states, gain_row):
    widened = states.astype(jnp.float32)
    spread = jnp.sqrt(jnp.mean(widened * widened, axis=-1, keepdims=True) + EPSILON)
    return ((widened / spread * gain_row).astype(jnp.bfloat16), spread)


def right_product(left, right):
    return lax.dot_general(
        left, right, (((1,), (1,)), ((), ())), preferred_element_type=jnp.float32
    )


def per_device(segment_in, norm_gains, projections, live_counts, cotangent):
    segment_pos = lax.axis_index("segment")
    model_index = lax.axis_index("mp")
    states = segment_in[0]
    gain_row = norm_gains[0]
    row_count, full_width = states.shape
    feature_width = cotangent.shape[1]
    w_primary = projections[0, :, 0, :]
    w_secondary = projections[0, :, 1, :]
    group_width = w_primary.shape[1]
    group_heads = group_width // DH
    normed, spread = normalize(states, gain_row)
    primary = jnp.dot(normed, w_primary, preferred_element_type=jnp.float32).astype(jnp.bfloat16)
    secondary = lax.cond(
        segment_pos == 0,
        lambda: jnp.dot(normed, w_secondary, preferred_element_type=jnp.float32).astype(
            jnp.bfloat16
        ),
        lambda: jnp.zeros_like(primary),
    )
    doc_keys, doc_values = from_behind((primary, secondary), "segment", 1)
    own_block = (doc_keys, doc_values, live_counts[0])
    window = [own_block]
    moving = own_block
    for offset in range(1, WIN):
        moving = from_behind((moving[0], moving[1], moving[2]), "blk", 1)
        window.append(moving)
    position = jnp.arange(row_count, dtype=jnp.int32)
    all_keys = jnp.concatenate([piece[0] for piece in window], 0).reshape(
        WIN * row_count, group_heads, DH
    )
    all_values = jnp.concatenate([piece[1] for piece in window], 0).reshape(
        WIN * row_count, group_heads, DH
    )
    key_live = jnp.concatenate([position < piece[2][0] for piece in window], 0)
    query_live = position < live_counts[1][0]
    query_heads = primary.reshape(row_count, group_heads, DH)
    scores = (
        jnp.einsum("qhd,khd->hqk", query_heads, all_keys, preferred_element_type=jnp.float32)
        * SCALE
    )
    scores = jnp.where(key_live[None, None, :], scores, NEGATIVE)
    row_max = jnp.max(scores, axis=-1, keepdims=True)
    expo = jnp.exp(scores - row_max)
    row_total = jnp.sum(expo, axis=-1, keepdims=True)
    softmax_out = expo / row_total
    weights_low = softmax_out.astype(jnp.bfloat16)
    attended = jnp.einsum(
        "hqk,khd->qhd", weights_low, all_values, preferred_element_type=jnp.float32
    ).astype(jnp.bfloat16)
    attended = jnp.where(query_live[:, None, None], attended, jnp.zeros_like(attended)).reshape(
        row_count, group_width
    )
    projected = lax.cond(
        segment_pos == 1,
        lambda: right_product(attended, w_secondary),
        lambda: jnp.zeros((row_count, full_width), jnp.float32),
    )
    layer_out = lax.psum_scatter(
        projected.astype(jnp.bfloat16), "mp", scatter_dimension=1, tiled=True
    )
    own_normed = lax.dynamic_slice_in_dim(normed, model_index * feature_width, feature_width, 1)
    segment_out = jnp.where(segment_pos == 0, own_normed, layer_out)[None]
    grad_out = jnp.dot(
        lax.all_gather(cotangent, "mp", axis=1, tiled=True),
        w_secondary,
        preferred_element_type=jnp.float32,
    )
    grad_out = grad_out.astype(jnp.bfloat16)
    grad_out = jnp.where(query_live[:, None], grad_out, jnp.zeros_like(grad_out))
    grad_heads = grad_out.reshape(row_count, group_heads, DH)
    grad_probs = jnp.einsum(
        "qhd,khd->hqk", grad_heads, all_values, preferred_element_type=jnp.float32
    )
    row_delta = jnp.sum(softmax_out * grad_probs, axis=-1, keepdims=True)
    grad_scores = (softmax_out * (grad_probs - row_delta)).astype(jnp.bfloat16)
    grad_queries = (
        (
            SCALE
            * jnp.einsum("hqk,khd->qhd", grad_scores, all_keys, preferred_element_type=jnp.float32)
        )
        .astype(jnp.bfloat16)
        .reshape(row_count, group_width)
    )
    key_parts = (
        SCALE
        * jnp.einsum("hqk,qhd->khd", grad_scores, query_heads, preferred_element_type=jnp.float32)
    ).reshape(WIN, row_count, group_width)
    value_parts = jnp.einsum(
        "hqk,qhd->khd", weights_low, grad_heads, preferred_element_type=jnp.float32
    ).reshape(WIN, row_count, group_width)
    key_total = key_parts[WIN - 1]
    value_total = value_parts[WIN - 1]
    for offset in range(WIN - 2, -1, -1):
        arrived = (
            from_behind(key_total.astype(jnp.bfloat16), "blk", -1).astype(key_total.dtype),
            from_behind(value_total.astype(jnp.bfloat16), "blk", -1).astype(value_total.dtype),
        )
        key_total = arrived[0] + key_parts[offset]
        value_total = arrived[1] + value_parts[offset]
    grad_keys = key_total.astype(jnp.bfloat16)
    grad_values = value_total.astype(jnp.bfloat16)
    back_keys, back_values = from_behind((grad_keys, grad_values), "segment", -1)
    partial_grad = lax.cond(
        segment_pos == 0,
        lambda: right_product(back_keys, w_primary) + right_product(back_values, w_secondary),
        lambda: right_product(grad_queries, w_primary),
    )
    widened = states.astype(jnp.float32)
    summed = lax.psum_scatter(
        partial_grad.astype(jnp.bfloat16), "mp", scatter_dimension=1, tiled=True
    ).astype(jnp.float32)
    own_states = lax.dynamic_slice_in_dim(widened, model_index * feature_width, feature_width, 1)
    own_gain = lax.dynamic_slice_in_dim(gain_row, model_index * feature_width, feature_width, 0)
    row_term = lax.psum(jnp.sum(summed * own_gain * own_states, axis=-1, keepdims=True), "mp")
    input_grad = (
        own_gain * summed / spread - own_states * row_term / (full_width * spread**3)
    ).astype(jnp.bfloat16)
    return (segment_out, input_grad[None])


def solution(mesh):
    in_specs = (
        P("segment", "blk", None),
        P("segment", None),
        P("segment", None, None, "mp"),
        P(None, "blk"),
        P("blk", "mp"),
    )
    out_specs = (P("segment", "blk", "mp"), P("segment", "blk", "mp"))
    return jax.shard_map(
        per_device, mesh=mesh, in_specs=in_specs, out_specs=out_specs, check_vma=False
    )
```

profile of v0, /device:TPU:2, one launch (start us, length us, event | category | flops | bytes accessed | tf_op | source)
XLA Modules:
  0.0 250.9 jit_solution(9817419102646836909)
XLA Ops:
  7.2 2.1 fusion.2
  9.3 17.6 %fusion.40 = (bf16[1,4096,1,512]{3,2,1,0:T(2,128)(2,1)}, bf16[1,4096,1,512]{3,2,1,0:T(2,128)(2,1)S(1)}) fusion(bf16[1,4096,2,512]{3,2,1,0:T(2,128)(2,1)} %param.13), kind=kLoop, calls=%fused_computation.70 | loop fusion | bytes 16777216 | tf_op jit(solution)/shard_map/slice | solution.py:40
  27.0 3.3 %copy.45 = bf16[1,4096,1,512]{3,1,2,0:T(8,128)(2,1)} copy(bf16[1,4096,1,512]{3,2,1,0:T(2,128)(2,1)S(1)} %get-tuple-element.63) | data formatting | bytes 8388608
  30.2 2.0 fusion.4
  33.7 4.6 %copy.44 = bf16[1,4096,1,512]{3,1,2,0:T(8,128)(2,1)S(1)} copy(bf16[1,4096,1,512]{3,2,1,0:T(2,128)(2,1)} %get-tuple-element.62) | data formatting | bytes 8388608
  41.5 2.7 %collective-permute-done = bf16[256,512]{1,0:T(8,128)(2,1)S(1)} collective-permute-done((bf16[256,512]{1,0:T(8,128)(2,1)S(1)}, bf16[256,512]{1,0:T(8,128)(2,1)S(1)}, u32[]{:S(2)}, u32[]{:S(2)}) %collective-permute-start) | collective-permute-done | bytes 262176 | tf_op jit(solution)/shard_map/ppermute | solution.py:18
  45.5 6.7 %collective-permute-done.7 = bf16[256,512]{1,0:T(8,128)(2,1)S(1)} collective-permute-done((bf16[256,512]{1,0:T(8,128)(2,1)S(1)}, bf16[256,512]{1,0:T(8,128)(2,1)S(1)}, u32[]{:S(2)}, u32[]{:S(2)}) %collective-permute-start.7) | collective-permute-done | bytes 262176 | tf_op jit(solution)/shard_map/ppermute | solution.py:18
  54.1 5.7 %collective-permute-start.4 = (s32[1]{0:T(128)}, s32[1]{0:T(128)}, u32[]{:S(2)}, u32[]{:S(2)}) collective-permute-start(s32[1]{0:T(128)} %bitcast.8), channel_id=1, source_target_pairs={{0,4},{4,8},{8,12},{12,16},{16,20},{20,24},{24,28},{28,32},{32,36}... | collective-permute-start | bytes 20 | tf_op jit(solution)/shard_map/ppermute | solution.py:18
  59.9 2.1 collective-permute-start.2
  62.7 4.8 %collective-permute-start.9 = (bf16[256,512]{1,0:T(8,128)(2,1)S(1)}, bf16[256,512]{1,0:T(8,128)(2,1)}, u32[]{:S(2)}, u32[]{:S(2)}) collective-permute-start(bf16[256,512]{1,0:T(8,128)(2,1)S(1)} %collective-permute-done.8), channel_id=1, source_target_pairs={{0,4},{4,8},{8,12},{12,16},{16,20},{20,24},{24,28},{28,32},{32,36}... | collective-permute-start | bytes 786440 | tf_op jit(solution)/shard_map/ppermute | solution.py:18
  70.7 6.3 %collective-permute-start.3 = (bf16[256,512]{1,0:T(8,128)(2,1)}, bf16[256,512]{1,0:T(8,128)(2,1)S(1)}, u32[]{:S(2)}, u32[]{:S(2)}) collective-permute-start(bf16[256,512]{1,0:T(8,128)(2,1)} %collective-permute-done.2), channel_id=1, source_target_pairs={{0,4},{4,8},{8,12},{12,16},{16,20},{20,24},{24,28},{28,32},{32,36}... | collective-permute-start | bytes 786440 | tf_op jit(solution)/shard_map/ppermute | solution.py:18
  77.8 2.5 collective-permute-start.6
  80.2 4.1 %collective-permute-start.10 = (bf16[256,512]{1,0:T(8,128)(2,1)}, bf16[256,512]{1,0:T(8,128)(2,1)}, u32[]{:S(2)}, u32[]{:S(2)}) collective-permute-start(bf16[256,512]{1,0:T(8,128)(2,1)} %collective-permute-done.9), channel_id=1, source_target_pairs={{0,4},{4,8},{8,12},{12,16},{16,20},{20,24},{24,28},{28,32},{32,36}... | collective-permute-start | bytes 786440 | tf_op jit(solution)/shard_map/ppermute | solution.py:18
  90.1 7.4 %fusion.44 = (f32[8,256]{1,0:T(8,128)S(1)}, f32[8,256,1024]{2,1,0:T(8,128)}) fusion(pred[1024]{0:T(1024)(128)(4,1)S(1)} %pad_add_fusion, bf16[256,8,64]{0,2,1:T(8,128)(2,1)S(1)} %bitcast.110, bf16[1024,8,64]{0,2,1:T(8,128)(2,1)} %bitcast.101), kind=kOutput, calls=%fused_computation.74 | convolution fusion | flops 276825088 | bytes 9708544 | tf_op jit(solution)/shard_map/sub | solution.py:76
  97.4 5.6 %fusion.25 = bf16[256,8,64]{0,2,1:T(8,128)(2,1)} fusion(bf16[1024,8,64]{0,2,1:T(8,128)(2,1)S(1)} %bitcast.112, f32[8,256,1024]{2,1,0:T(8,128)} %get-tuple-element.75, f32[8,256]{1,0:T(8,128)S(1)} %get-tuple-element.74), kind=kOutput, calls=%fused_computation.35 | convolution fusion | flops 272760832 | bytes 9707520 | tf_op jit(solution)/shard_map/hqk,khd->qhd/dot_general | solution.py:80
  103.0 6.4 %conditional.4 = (bf16[256,4096]{1,0:T(8,128)(2,1)}) conditional(s32[]{:T(128)} %convert_element_type.109, () %tuple.26, (s32[]{:T(128)}, s32[256,1,1]{0,2,1:T(1,128)S(1)}, bf16[256,8,64]{0,2,1:T(8,128)(2,1)}, bf16[4096,512]{1,0:T(8,128)(2,1)}) %tuple.59), branch_computations={%region_5.6_spmd, %region_6.7_spmd} | conditional | flops 1073873152 | bytes 7079436 | solution.py:86
  104.5 4.9 %fusion.47 = bf16[256,4096]{1,0:T(8,128)(2,1)} fusion(bf16[256,512]{0,1:T(8,128)(2,1)S(1)} %bitcast.109, bf16[4096,512]{1,0:T(8,128)(2,1)} %get-tuple-element.47), kind=kOutput, calls=%fused_computation.77 | convolution fusion | flops 1073741824 | bytes 6553600 | tf_op jit(solution)/shard_map/cond/branch_1_fun/dot_general | solution.py:28
  109.5 4.8 %fusion.29 = bf16[256,512]{1,0:T(8,128)(2,1)} fusion(bf16[256,4096]{1,0:T(8,128)(2,1)} %all-gather.2.cloned.1.call-done, bf16[4096,512]{1,0:T(8,128)(2,1)} %bitcast.97, pred[256]{0:T(512)(128)(4,1)S(1)} %iota_compare_fusion), kind=kOutput, calls=%fused_computation.37 | convolution fusion | flops 1074003968 | bytes 6553856 | tf_op jit(solution)/shard_map/dot_general | solution.py:96
  116.1 5.1 %multiply_reduce_fusion = (f32[8,256]{1,0:T(8,128)S(1)}, f32[8,256,1024]{2,1,0:T(8,128)S(1)}) fusion(f32[8,256,1024]{2,1,0:T(8,128)} %get-tuple-element.75, f32[8,256]{1,0:T(8,128)S(1)} %get-tuple-element.74, bf16[256,8,64]{0,2,1:T(8,128)(2,1)} %bitcast.117, bf16[1024,8,64]{0,2,1:T(8,128)(2,1)S(1)} %bitcast.113), kind=kOutput, calls=%fused_computation.6 | convolution fusion | flops 274724864 | bytes 18104320 | tf_op jit(solution)/shard_map/qhd,khd->hqk/dot_general | solution.py:104
  129.1 4.6 %fusion.15 = f32[1024,8,64]{0,2,1:T(8,128)S(1)} fusion(bf16[256,8,64]{0,2,1:T(8,128)(2,1)S(1)} %bitcast.118, f32[8,256,1024]{2,1,0:T(8,128)} %get-tuple-element.75, f32[8,256]{1,0:T(8,128)S(1)} %get-tuple-element.74), kind=kOutput, calls=%fused_computation.29 | convolution fusion | flops 272629760 | bytes 10756096 | tf_op jit(solution)/shard_map/hqk,qhd->khd/dot_general | solution.py:121
  137.4 2.5 %fusion.42 = (f32[256,8,64]{0,2,1:T(8,128)S(1)}, f32[256,8,64]{0,2,1:T(8,128)}, f32[256,8,64]{0,2,1:T(8,128)}) fusion(f32[1024,8,64]{0,2,1:T(8,128)} %copy-done.5), kind=kLoop, calls=%fused_computation.72 | loop fusion | bytes 3145728 | tf_op jit(solution)/shard_map/slice | solution.py:131
  148.2 2.2 copy.34
  167.4 3.6 %fusion.28 = bf16[256,8,64]{0,2,1:T(8,128)(2,1)S(1)} fusion(bf16[1024,8,64]{0,2,1:T(8,128)(2,1)S(1)} %bitcast.102, bf16[8,256,1024]{2,1,0:T(8,128)(2,1)} %copy-done.3), kind=kOutput, calls=%fused_computation.36 | convolution fusion | flops 268697600 | bytes 5505024 | tf_op jit(solution)/shard_map/hqk,khd->qhd/dot_general | solution.py:112
  171.0 2.3 collective-permute-done.14
  173.3 5.6 %collective-permute-done.18 = bf16[256,512]{1,0:T(8,128)(2,1)S(1)} collective-permute-done((bf16[256,512]{1,0:T(8,128)(2,1)S(1)}, bf16[256,512]{1,0:T(8,128)(2,1)S(1)}, u32[]{:S(2)}, u32[]{:S(2)}) %collective-permute-start.18) | collective-permute-done | bytes 262176 | tf_op jit(solution)/shard_map/ppermute | solution.py:18
  178.9 2.7 %conditional.5 = (bf16[256,4096]{1,0:T(8,128)(2,1)}) conditional(s32[]{:T(128)} %convert_element_type.110, (bf16[256,8,64]{0,2,1:T(8,128)(2,1)S(1)}, bf16[4096,512]{1,0:T(8,128)(2,1)S(1)}) %tuple.56, (bf16[256,512]{1,0:T(8,128)(2,1)S(1)}, bf16[4096,512]{1,0:T(8,128)(2,1)S(1)}, bf16[256,512]{1,0:T(8,128)(2,1)S(1)}, ...), branch_computations={%region_9.10_spmd, %region_10.11_spmd} | conditional | flops 2149580800 | bytes 39321720 | solution.py:136
  178.9 2.7 %fusion.45 = bf16[256,4096]{1,0:T(8,128)(2,1)} fusion(bf16[256,512]{0,1:T(8,128)(2,1)S(1)} %bitcast.116, bf16[4096,512]{1,0:T(8,128)(2,1)S(1)} %get-tuple-element.49), kind=kOutput, calls=%fused_computation.75 | convolution fusion | flops 1073741824 | bytes 6553600 | tf_op jit(solution)/shard_map/cond/branch_0_fun/dot_general | solution.py:28
  181.7 2.5 convert_element_type.106
  184.1 2.2 select_bitcast_fusion
  186.3 45.4 %reduce-scatter.5.cloned.1.call-done = bf16[256,1024]{1,0:T(8,128)(2,1)} async-done(((bf16[256,4096]{1,0:T(8,128)(2,1)}), bf16[256,1024]{1,0:T(8,128)(2,1)}) %reduce-scatter.5.cloned.1.call-update) | async-done | bytes 524304 | tf_op jit(solution)/shard_map/reduce_scatter | solution.py:142
  233.3 8.6 %psum.7 = f32[256]{0:T(256)S(1)} all-reduce(f32[256]{0:T(256)S(1)} %fusion.30), channel_id=1, replica_groups=mesh['segment'=2,'blk'=32,'mp'=4] {'mp'}, use_global_device_ids=true, to_apply=%region_13.14 | all-reduce | flops 256 | bytes 2048 | tf_op jit(solution)/shard_map/psum | solution.py:147
  241.9 2.4 fusion.36
  (113 shorter events, 59.9 us)
Async XLA Ops:
  7.2 102.3 %all-gather.2.cloned.1.call-start = ((), (), s32[]{:S(2)}) async-start(), calls=%async_computation.3 | async-start | bytes 2621440 | tf_op jit(solution)/shard_map/all_gather | solution.py:97
  32.3 11.9 %collective-permute-start = (bf16[256,512]{1,0:T(8,128)(2,1)S(1)}, bf16[256,512]{1,0:T(8,128)(2,1)S(1)}, u32[]{:S(2)}, u32[]{:S(2)}) collective-permute-start(bf16[256,512]{1,0:T(8,128)(2,1)S(1)} %get-tuple-element.78), channel_id=1, source_target_pairs={{0,128},{1,129},{2,130},{3,131},{4,132},{5,133},{6,134},{7,135},{8... | collective-permute-start | bytes 786440 | tf_op jit(solution)/shard_map/ppermute | solution.py:18
  33.6 150.5 %reduce-scatter.3.cloned.1.call-start = ((), (), s32[]{:S(2)}) async-start(), calls=%async_computation.2 | async-start | bytes 2621440 | tf_op jit(solution)/shard_map/reduce_scatter | solution.py:91
  38.3 15.2 %copy-start.19 = (s32[2,1]{0,1:T(1,128)S(1)}, s32[2,1]{0,1:T(1,128)}, u32[]{:S(2)}) copy-start(s32[2,1]{0,1:T(1,128)} %param.14) | copy-start | bytes 28
  40.2 12.0 %collective-permute-start.7 = (bf16[256,512]{1,0:T(8,128)(2,1)S(1)}, bf16[256,512]{1,0:T(8,128)(2,1)S(1)}, u32[]{:S(2)}, u32[]{:S(2)}) collective-permute-start(bf16[256,512]{1,0:T(8,128)(2,1)S(1)} %fusion.22), channel_id=1, source_target_pairs={{0,128},{1,129},{2,130},{3,131},{4,132},{5,133},{6,134},{7,135},{8... | collective-permute-start | bytes 786440 | tf_op jit(solution)/shard_map/ppermute | solution.py:18
  44.2 40.7 %copy-start.12 = (bf16[256,512]{1,0:T(8,128)(2,1)}, bf16[256,512]{1,0:T(8,128)(2,1)S(1)}, u32[]{:S(2)}) copy-start(bf16[256,512]{1,0:T(8,128)(2,1)S(1)} %collective-permute-done) | copy-start | bytes 786436
  44.2 15.7 %collective-permute-start.1 = (bf16[256,512]{1,0:T(8,128)(2,1)S(1)}, bf16[256,512]{1,0:T(8,128)(2,1)S(1)}, u32[]{:S(2)}, u32[]{:S(2)}) collective-permute-start(bf16[256,512]{1,0:T(8,128)(2,1)S(1)} %collective-permute-done), channel_id=1, source_target_pairs={{0,4},{4,8},{8,12},{12,16},{16,20},{20,24},{24,28},{28,32},{32,36}... | collective-permute-start | bytes 786440 | tf_op jit(solution)/shard_map/ppermute | solution.py:18
  52.2 15.8 %copy-start.13 = (bf16[256,512]{1,0:T(8,128)(2,1)}, bf16[256,512]{1,0:T(8,128)(2,1)S(1)}, u32[]{:S(2)}) copy-start(bf16[256,512]{1,0:T(8,128)(2,1)S(1)} %collective-permute-done.7) | copy-start | bytes 786436
  52.2 10.5 %collective-permute-start.8 = (bf16[256,512]{1,0:T(8,128)(2,1)S(1)}, bf16[256,512]{1,0:T(8,128)(2,1)S(1)}, u32[]{:S(2)}, u32[]{:S(2)}) collective-permute-start(bf16[256,512]{1,0:T(8,128)(2,1)S(1)} %collective-permute-done.7), channel_id=1, source_target_pairs={{0,4},{4,8},{8,12},{12,16},{16,20},{20,24},{24,28},{28,32},{32,36}... | collective-permute-start | bytes 786440 | tf_op jit(solution)/shard_map/ppermute | solution.py:18
  54.1 14.0 %collective-permute-start.4 = (s32[1]{0:T(128)}, s32[1]{0:T(128)}, u32[]{:S(2)}, u32[]{:S(2)}) collective-permute-start(s32[1]{0:T(128)} %bitcast.8), channel_id=1, source_target_pairs={{0,4},{4,8},{8,12},{12,16},{16,20},{20,24},{24,28},{28,32},{32,36}... | collective-permute-start | bytes 20 | tf_op jit(solution)/shard_map/ppermute | solution.py:18
  59.9 25.1 %copy-start.15 = (bf16[256,512]{1,0:T(8,128)(2,1)}, bf16[256,512]{1,0:T(8,128)(2,1)S(1)}, u32[]{:S(2)}) copy-start(bf16[256,512]{1,0:T(8,128)(2,1)S(1)} %collective-permute-done.1) | copy-start | bytes 786436
  59.9 10.8 %collective-permute-start.2 = (bf16[256,512]{1,0:T(8,128)(2,1)S(1)}, bf16[256,512]{1,0:T(8,128)(2,1)}, u32[]{:S(2)}, u32[]{:S(2)}) collective-permute-start(bf16[256,512]{1,0:T(8,128)(2,1)S(1)} %collective-permute-done.1), channel_id=1, source_target_pairs={{0,4},{4,8},{8,12},{12,16},{16,20},{20,24},{24,28},{28,32},{32,36}... | collective-permute-start | bytes 786440 | tf_op jit(solution)/shard_map/ppermute | solution.py:18
  62.7 22.3 %copy-start.14 = (bf16[256,512]{1,0:T(8,128)(2,1)}, bf16[256,512]{1,0:T(8,128)(2,1)S(1)}, u32[]{:S(2)}) copy-start(bf16[256,512]{1,0:T(8,128)(2,1)S(1)} %collective-permute-done.8) | copy-start | bytes 786436
  62.7 17.5 %collective-permute-start.9 = (bf16[256,512]{1,0:T(8,128)(2,1)S(1)}, bf16[256,512]{1,0:T(8,128)(2,1)}, u32[]{:S(2)}, u32[]{:S(2)}) collective-permute-start(bf16[256,512]{1,0:T(8,128)(2,1)S(1)} %collective-permute-done.8), channel_id=1, source_target_pairs={{0,4},{4,8},{8,12},{12,16},{16,20},{20,24},{24,28},{28,32},{32,36}... | collective-permute-start | bytes 786440 | tf_op jit(solution)/shard_map/ppermute | solution.py:18
  68.2 8.9 %collective-permute-start.5 = (s32[1]{0:T(128)}, s32[1]{0:T(128)}, u32[]{:S(2)}, u32[]{:S(2)}) collective-permute-start(s32[1]{0:T(128)} %collective-permute-done.4), channel_id=1, source_target_pairs={{0,4},{4,8},{8,12},{12,16},{16,20},{20,24},{24,28},{28,32},{32,36}... | collective-permute-start | bytes 20 | tf_op jit(solution)/shard_map/ppermute | solution.py:18
  70.7 14.3 %collective-permute-start.3 = (bf16[256,512]{1,0:T(8,128)(2,1)}, bf16[256,512]{1,0:T(8,128)(2,1)S(1)}, u32[]{:S(2)}, u32[]{:S(2)}) collective-permute-start(bf16[256,512]{1,0:T(8,128)(2,1)} %collective-permute-done.2), channel_id=1, source_target_pairs={{0,4},{4,8},{8,12},{12,16},{16,20},{20,24},{24,28},{28,32},{32,36}... | collective-permute-start | bytes 786440 | tf_op jit(solution)/shard_map/ppermute | solution.py:18
  77.8 6.5 %collective-permute-start.6 = (s32[1]{0:T(128)}, s32[1]{0:T(128)}, u32[]{:S(2)}, u32[]{:S(2)}) collective-permute-start(s32[1]{0:T(128)} %collective-permute-done.5), channel_id=1, source_target_pairs={{0,4},{4,8},{8,12},{12,16},{16,20},{20,24},{24,28},{28,32},{32,36}... | collective-permute-start | bytes 20 | tf_op jit(solution)/shard_map/ppermute | solution.py:18
  80.2 7.3 %collective-permute-start.10 = (bf16[256,512]{1,0:T(8,128)(2,1)}, bf16[256,512]{1,0:T(8,128)(2,1)}, u32[]{:S(2)}, u32[]{:S(2)}) collective-permute-start(bf16[256,512]{1,0:T(8,128)(2,1)} %collective-permute-done.9), channel_id=1, source_target_pairs={{0,4},{4,8},{8,12},{12,16},{16,20},{20,24},{24,28},{28,32},{32,36}... | collective-permute-start | bytes 786440 | tf_op jit(solution)/shard_map/ppermute | solution.py:18
  90.1 7.4 %copy-start.9 = (bf16[1024,512]{0,1:T(8,128)(2,1)S(1)}, bf16[1024,512]{0,1:T(8,128)(2,1)}, u32[]{:S(2)}) copy-start(bf16[1024,512]{0,1:T(8,128)(2,1)} %copy.27) | copy-start | bytes 3145732
  109.4 122.3 %reduce-scatter.5.cloned.1.call-start = ((), (), s32[]{:S(2)}) async-start(), calls=%async_computation.4 | async-start | bytes 2621440 | tf_op jit(solution)/shard_map/reduce_scatter | solution.py:142
  116.1 5.1 %slice-start = ((s8[8388608]{0:T(1024)(128)(4,1)}), s8[4194304]{0:T(1024)(128)(4,1)S(1)}, s32[]{:S(2)}) async-start(s8[8388608]{0:T(1024)(128)(4,1)} %bitcast.99), calls=%async_computation.5 | async-start | bytes 8388608
  116.1 5.9 %slice-start.1 = ((s8[8388608]{0:T(1024)(128)(4,1)}), s8[4194304]{0:T(1024)(128)(4,1)S(1)}, s32[]{:S(2)}) async-start(s8[8388608]{0:T(1024)(128)(4,1)} %bitcast.99), calls=%async_computation.6 | async-start | bytes 8388608
  127.8 14.7 %collective-permute-start.11 = (bf16[256,512]{1,0:T(8,128)(2,1)S(1)}, bf16[256,512]{1,0:T(8,128)(2,1)}, u32[]{:S(2)}, u32[]{:S(2)}) collective-permute-start(bf16[256,512]{1,0:T(8,128)(2,1)S(1)} %copy.32), channel_id=1, source_target_pairs={{4,0},{8,4},{12,8},{16,12},{20,16},{24,20},{28,24},{32,28},{36,32}... | collective-permute-start | bytes 786440 | tf_op jit(solution)/shard_map/ppermute | solution.py:18
  136.0 8.9 %collective-permute-start.15 = (bf16[256,512]{1,0:T(8,128)(2,1)}, bf16[256,512]{1,0:T(8,128)(2,1)}, u32[]{:S(2)}, u32[]{:S(2)}) collective-permute-start(bf16[256,512]{1,0:T(8,128)(2,1)} %copy.36), channel_id=1, source_target_pairs={{4,0},{8,4},{12,8},{16,12},{20,16},{24,20},{28,24},{32,28},{36,32}... | collective-permute-start | bytes 786440 | tf_op jit(solution)/shard_map/ppermute | solution.py:18
  143.6 8.8 %collective-permute-start.12 = (bf16[256,512]{1,0:T(8,128)(2,1)S(1)}, bf16[256,512]{1,0:T(8,128)(2,1)}, u32[]{:S(2)}, u32[]{:S(2)}) collective-permute-start(bf16[256,512]{1,0:T(8,128)(2,1)S(1)} %add_convert_fusion.5), channel_id=1, source_target_pairs={{4,0},{8,4},{12,8},{16,12},{20,16},{24,20},{28,24},{32,28},{36,32}... | collective-permute-start | bytes 786440 | tf_op jit(solution)/shard_map/ppermute | solution.py:18
  146.6 8.2 %collective-permute-start.16 = (bf16[256,512]{1,0:T(8,128)(2,1)}, bf16[256,512]{1,0:T(8,128)(2,1)}, u32[]{:S(2)}, u32[]{:S(2)}) collective-permute-start(bf16[256,512]{1,0:T(8,128)(2,1)} %add_convert_fusion.2), channel_id=1, source_target_pairs={{4,0},{8,4},{12,8},{16,12},{20,16},{24,20},{28,24},{32,28},{36,32}... | collective-permute-start | bytes 786440 | tf_op jit(solution)/shard_map/ppermute | solution.py:18
  148.2 19.2 %copy-start.6 = (bf16[1024,512]{0,1:T(8,128)(2,1)S(1)}, bf16[1024,512]{0,1:T(8,128)(2,1)}, u32[]{:S(2)}) copy-start(bf16[1024,512]{0,1:T(8,128)(2,1)} %copy.30) | copy-start | bytes 3145732
  153.6 8.5 %collective-permute-start.13 = (bf16[256,512]{1,0:T(8,128)(2,1)S(1)}, bf16[256,512]{1,0:T(8,128)(2,1)}, u32[]{:S(2)}, u32[]{:S(2)}) collective-permute-start(bf16[256,512]{1,0:T(8,128)(2,1)S(1)} %add_convert_fusion.4), channel_id=1, source_target_pairs={{4,0},{8,4},{12,8},{16,12},{20,16},{24,20},{28,24},{32,28},{36,32}... | collective-permute-start | bytes 786440 | tf_op jit(solution)/shard_map/ppermute | solution.py:18
  156.7 8.1 %collective-permute-start.17 = (bf16[256,512]{1,0:T(8,128)(2,1)}, bf16[256,512]{1,0:T(8,128)(2,1)}, u32[]{:S(2)}, u32[]{:S(2)}) collective-permute-start(bf16[256,512]{1,0:T(8,128)(2,1)} %add_convert_fusion.1), channel_id=1, source_target_pairs={{4,0},{8,4},{12,8},{16,12},{20,16},{24,20},{28,24},{32,28},{36,32}... | collective-permute-start | bytes 786440 | tf_op jit(solution)/shard_map/ppermute | solution.py:18
  162.1 16.8 %copy-start.1 = (bf16[1,4096,1,512]{3,1,2,0:T(8,128)(2,1)S(1)}, bf16[1,4096,1,512]{3,1,2,0:T(8,128)(2,1)}, u32[]{:S(2)}) copy-start(bf16[1,4096,1,512]{3,1,2,0:T(8,128)(2,1)} %copy-done) | copy-start | bytes 12582916
  163.4 9.9 %collective-permute-start.14 = (bf16[256,512]{1,0:T(8,128)(2,1)S(1)}, bf16[256,512]{1,0:T(8,128)(2,1)S(1)}, u32[]{:S(2)}, u32[]{:S(2)}) collective-permute-start(bf16[256,512]{1,0:T(8,128)(2,1)S(1)} %add_convert_fusion.3), channel_id=1, source_target_pairs={{128,0},{129,1},{130,2},{131,3},{132,4},{133,5},{134,6},{135,7},{1... | collective-permute-start | bytes 786440 | tf_op jit(solution)/shard_map/ppermute | solution.py:18
  166.1 12.8 %collective-permute-start.18 = (bf16[256,512]{1,0:T(8,128)(2,1)S(1)}, bf16[256,512]{1,0:T(8,128)(2,1)S(1)}, u32[]{:S(2)}, u32[]{:S(2)}) collective-permute-start(bf16[256,512]{1,0:T(8,128)(2,1)S(1)} %add_convert_fusion), channel_id=1, source_target_pairs={{128,0},{129,1},{130,2},{131,3},{132,4},{133,5},{134,6},{135,7},{1... | collective-permute-start | bytes 786440 | tf_op jit(solution)/shard_map/ppermute | solution.py:18
  (8 other events, 20.9 us)
Sparse Core Ops, SparseCore 0:
  33.7 40.4 all-gather.1
  109.6 36.7 reduce-scatter.2
  181.8 49.9 reduce-scatter.4
where the time goes:
time: 252 us; the launch traced here: 251 us
  waiting for transfers between devices  62.9 us (25%)
  local copies, waits for them, and re-layouts  51.3 us (20%)
  starting transfers between devices  43.4 us (17%)
  matrix products  40.7 us (16%)
  other arithmetic  29.7 us (12%)
  between operations  14.2 us (6%)
  blocking collectives  8.58 us (3%)
    reduce_scatter x1, waiting for transfers between devices, per_device(): lax.psum_scatter(partial_grad.astype(jnp.bfloat16), 'mp', scatter_dimensi...  45.4 us
    ppermute x19, starting transfers between devices, from_behind(): return lax.ppermute(x, axis, pairs)  43.3 us
    slice x1, local copies, waits for them, and re-layouts, per_device(): w_primary = projections[0, :, 0, :]  17.6 us
    ppermute x19, waiting for transfers between devices, from_behind(): return lax.ppermute(x, axis, pairs)  17.4 us
    unnamed x38, local copies, waits for them, and re-layouts  14.1 us
    psum x1, blocking collectives, per_device(): lax.psum(jnp.sum(summed * own_gain * own_states, axis=-1, keepdims=True),...  8.58 us
    dot_general x2, matrix products, right_product(): lax.dot_general(left, right, (((1,), (1,)), ((), ())), preferred_element_...  7.59 us
    sub x1, matrix products, per_device(): expo = jnp.exp(scores - row_max)  7.37 us
  transfers between devices with their start and end apart: 22, of which 5 were waited for; matrix products, arithmetic and copies ran while one was open for 34% of the time, Pallas kernels for 0%

commit v1 on v0

v1 whole, which is shorter than its diff:
```python
import jax
import jax.numpy as jnp
from jax import lax
from jax.experimental import pallas as pl
from jax.experimental.pallas import tpu as pltpu
from jax.sharding import PartitionSpec as P

MESH = pl.DeviceIdType.MESH
F32 = jnp.float32
BF16 = jnp.bfloat16
EPSILON = 1e-06
SCALE = 0.125
NEGATIVE = -1e30
NT = (((1,), (1,)), ((), ()))
TN = (((0,), (0,)), ((), ()))
ROWS = 256
HALF = 128
WIDTH = 4096
SLICE = 1024
GROUP = 512
SLAB = ROWS + 16


def kernel(
    live_ref, x_hbm, gain_hbm, w_hbm, cot_hbm,
    seg_hbm, grad_hbm,
    states, gains, normed, rspread, wraw, wcat, acc, cot,
    kvsend, qsend, dsend, docs, qbuf, dbuf,
    sbuf, pbuf, dpbuf, gacc, osend, dqsend, obuf, dqbuf,
    zout, zin, gout, gbuf,
    left, lpart, lfar, lin, gpart, gfar, gin,
    rterm, rsend, rin, lout, gfin,
    load_sem, w_sem, loc_sem, out_sem,
    cot_s, cot_r, kv_s, doc_r, q_s, q_r, d_s, d_r, z_s, z_r,
    o_s, o_r, dq_s, dq_r, zg_s, zg_r, g_s, g_r,
    l_s, l_r, rs_s, rs_r, rt_s, rt_r,
):
    seg = lax.axis_index("segment")
    blk = lax.axis_index("blk")
    mp = lax.axis_index("mp")
    z = blk // 4
    quad = lax.rem(blk, 4)
    me = seg * 4 + quad
    n_z = lax.axis_size("blk") // 4
    z_up = lax.rem(z + 1, n_z)
    z_dn = lax.rem(z + n_z - 1, n_z)
    y_r, y_l, y_far = lax.rem(mp + 1, 4), lax.rem(mp + 3, 4), lax.rem(mp + 2, 4)

    def peer(t):
        return (t // 4, z * 4 + lax.rem(t, 4), mp)

    def at_y(y):
        return (seg, blk, y)

    def at_z(zz):
        return (seg, zz * 4 + quad, mp)

    def remote(src, dst, send, recv, to):
        return pltpu.make_async_remote_copy(
            src_ref=src, dst_ref=dst, send_sem=send, recv_sem=recv,
            device_id=to, device_id_type=MESH,
        )

    x_load = pltpu.make_async_copy(x_hbm.at[0], states, load_sem.at[0])
    g_load = pltpu.make_async_copy(gain_hbm, gains, load_sem.at[1])
    c_load = pltpu.make_async_copy(cot_hbm, cot.at[mp], load_sem.at[2])
    x_load.start()
    g_load.start()

    @pl.when(seg == 1)
    def _():
        c_load.start()

    def w_load(c):
        rows = pl.ds(pl.multiple_of(c * SLICE, SLICE), SLICE)
        return pltpu.make_async_copy(w_hbm.at[0, rows], wraw.at[rows], w_sem.at[c])

    for c in range(4):
        w_load(c).start()

    barrier = pltpu.get_barrier_semaphore()
    for k in range(1, 8):
        pl.semaphore_signal(barrier, inc=1, device_id=peer(lax.rem(me + k, 8)), device_id_type=MESH)
    for to in (at_y(y_r), at_y(y_l), at_y(y_far), at_z(z_up), at_z(z_dn)):
        pl.semaphore_signal(barrier, inc=1, device_id=to, device_id_type=MESH)
    pl.semaphore_wait(barrier, 12)

    top, bottom = pl.ds(0, HALF), pl.ds(HALF, HALF)

    def cot_copy(n):
        own_r = lambda h: (cot.at[mp, h], at_y(y_r))
        own_l = lambda h: (cot.at[mp, h], at_y(y_l))
        ref, to = [
            own_r(top), own_r(bottom), own_l(bottom), own_l(top),
            (cot.at[y_l, top], at_y(y_r)), (cot.at[y_r, bottom], at_y(y_l)),
        ][n]
        return remote(ref, ref, cot_s.at[n], cot_r.at[n], to)

    def cot_recv(n):
        ref = [
            cot.at[y_l, top], cot.at[y_l, bottom], cot.at[y_r, bottom], cot.at[y_r, top],
            cot.at[y_far, top], cot.at[y_far, bottom],
        ][n]
        remote(ref, ref, cot_s.at[n], cot_r.at[n], at_y(y_r)).wait_recv()

    @pl.when(seg == 1)
    def _():
        c_load.wait()
        for n in (0, 2, 1, 3):
            cot_copy(n).start()

    x_load.wait()
    g_load.wait()

    @pl.loop(0, 8)
    def _(i):
        rows = pl.ds(pl.multiple_of(i * 32, 32), 32)
        x = states[rows].astype(F32)
        inverse = 1.0 / jnp.sqrt(jnp.mean(x * x, axis=-1, keepdims=True) + EPSILON)
        rspread[rows] = jnp.broadcast_to(inverse, (32, 128))
        normed[rows] = (x * inverse * gains[...]).astype(BF16)

    own_columns = pl.ds(pl.multiple_of(mp * SLICE, SLICE), SLICE)
    normed_out = pltpu.make_async_copy(normed.at[:, own_columns], seg_hbm.at[0], out_sem.at[0])

    @pl.when(seg == 0)
    def _():
        normed_out.start()

    acc[...] = jnp.zeros_like(acc)

    @pl.loop(0, 4)
    def _(c):
        w_load(c).wait()

        @pl.loop(0, 4)
        def _(j):
            rows = pl.ds(pl.multiple_of(c * SLICE + j * 256, 256), 256)
            wcat[rows] = wraw[rows].reshape(256, 2 * GROUP)

        rows = pl.ds(pl.multiple_of(c * SLICE, SLICE), SLICE)

        @pl.when(seg == 0)
        def _():
            acc[...] += jnp.dot(normed[:, rows], wcat[rows], preferred_element_type=F32)

        @pl.when(seg == 1)
        def _():
            acc[:, :GROUP] += jnp.dot(
                normed[:, rows], wcat[rows, :GROUP], preferred_element_type=F32
            )

    def low_half(rows):
        return lax.broadcasted_iota(jnp.int32, (rows, 128), 1) < 64

    def exchange(a, b):
        low = low_half(a.shape[0])
        return jnp.where(low, a, pltpu.roll(b, 64, 1)), jnp.where(low, pltpu.roll(a, 64, 1), b)

    row_live = lax.broadcasted_iota(jnp.int32, (ROWS, 128), 0) < live_ref[1, 0]

    def kv_copy(t):
        return remote(kvsend.at[t], docs.at[3 + quad], kv_s.at[t], doc_r.at[3 + quad], peer(t))

    def q_copy(t):
        return remote(qsend.at[t], qbuf.at[quad], q_s.at[t], q_r.at[quad], peer(t))

    def d_copy(t):
        return remote(dsend.at[t], dbuf.at[quad], d_s.at[t], d_r.at[quad], peer(t))

    kv_own = pltpu.make_async_copy(kvsend.at[me], docs.at[3 + quad], loc_sem.at[0])
    q_own = pltpu.make_async_copy(qsend.at[me], qbuf.at[quad], loc_sem.at[0])
    d_own = pltpu.make_async_copy(dsend.at[me], dbuf.at[quad], loc_sem.at[1])

    @pl.when(seg == 0)
    def _():
        count = jnp.full((16, 128), live_ref[0, 0], jnp.int32).astype(F32).astype(BF16)
        for g in range(4):
            keys = acc[:, g * 128:(g + 1) * 128]
            values = acc[:, GROUP + g * 128:GROUP + (g + 1) * 128]
            even, odd = exchange(keys, values)
            kvsend[2 * g, :ROWS] = even.astype(BF16)
            kvsend[2 * g + 1, :ROWS] = odd.astype(BF16)
            kvsend[2 * g, ROWS:] = count
            kvsend[2 * g + 1, ROWS:] = count
        for k in range(1, 8):
            kv_copy(lax.rem(me + k, 8)).start()
        kv_own.start()

    @pl.when(seg == 1)
    def _():
        for g in range(4):
            pair = acc[:, g * 128:(g + 1) * 128]
            even, odd = exchange(pair[:HALF], pair[HALF:])
            qsend[2 * g] = even.astype(BF16)
            qsend[2 * g + 1] = odd.astype(BF16)
        for k in range(1, 8):
            q_copy(lax.rem(me + k, 8)).start()
        q_own.start()
        cot_recv(0)
        cot_copy(4).start()
        cot_recv(2)
        cot_copy(5).start()

    def z_copy(s):
        return remote(docs.at[s + 4], docs.at[s], z_s.at[s], z_r.at[s], at_z(z_up))

    def z_recv(s):
        remote(docs.at[s], docs.at[s], z_s.at[s], z_r.at[s], at_z(z_up)).wait_recv()

    for j in (1, 2, 3, 0):
        @pl.when(me == j)
        def _():
            kv_own.wait()

        @pl.when(me != j)
        def _():
            remote(docs.at[3 + j], docs.at[3 + j], kv_s.at[0], doc_r.at[3 + j], peer(j)).wait_recv()

        if j > 0:
            z_copy(j - 1).start()

    def from_summary(buf, recv, own, i):
        @pl.when(me == 4 + i)
        def _():
            own.wait()

        @pl.when(me != 4 + i)
        def _():
            remote(buf.at[i], buf.at[i], recv.at[i], recv.at[i], peer(4 + i)).wait_recv()

    def query(i):
        slab = qbuf[i].astype(F32)
        low = low_half(HALF)
        a = jnp.where(low, slab, 0.0)
        b = jnp.where(low, pltpu.roll(slab, 64, 1), 0.0)
        return jnp.concatenate([a, b], 0).astype(BF16)

    def gradient(i):
        slab = dbuf[i].astype(F32)
        low = low_half(HALF)
        a = jnp.where(low, 0.0, pltpu.roll(slab, 64, 1))
        b = jnp.where(low, 0.0, slab)
        return jnp.concatenate([a, b], 0).astype(BF16)

    def o_copy(i):
        return remote(osend.at[i], obuf.at[me], o_s.at[i], o_r.at[me], peer(4 + i))

    def dq_copy(i):
        return remote(dqsend.at[i], dqbuf.at[me], dq_s.at[i], dq_r.at[me], peer(4 + i))

    def o_own(i):
        return pltpu.make_async_copy(osend.at[i], obuf.at[me], loc_sem.at[2])

    def dq_own(i):
        return pltpu.make_async_copy(dqsend.at[i], dqbuf.at[me], loc_sem.at[3])

    @pl.loop(0, 4)
    def _(n):
        i = 3 - n

        @pl.when(i < 3)
        def _():
            z_recv(i)

        from_summary(qbuf, q_r, q_own, i)
        q0 = query(i)
        position = lax.broadcasted_iota(jnp.int32, (ROWS, ROWS), 0).astype(F32)
        peak = jnp.full((1, ROWS), NEGATIVE, F32)
        for j in range(4):
            s = lax.dot_general(docs[i + j, :ROWS], q0, NT, preferred_element_type=F32) * SCALE
            count = docs[i + j, ROWS:].astype(F32)[:1]
            count = jnp.where(4 * z - 3 + i + j >= 0, count, 0.0)
            count = jnp.concatenate([count, count], 1)
            s = jnp.where(position < count, s, NEGATIVE)
            sbuf[i, j] = s
            peak = jnp.maximum(peak, jnp.max(s, axis=0, keepdims=True))
        total = jnp.zeros((1, ROWS), F32)
        for j in range(4):
            e = jnp.exp(sbuf[i, j] - peak)
            sbuf[i, j] = e
            total = total + jnp.sum(e, axis=0, keepdims=True)
        share = 1.0 / total
        out = jnp.zeros((128, ROWS), F32)
        for j in range(4):
            probs = sbuf[i, j] * share
            sbuf[i, j] = probs
            low = probs.astype(BF16)
            pbuf[i, j] = low
            out = out + lax.dot_general(docs[i + j, :ROWS], low, TN, preferred_element_type=F32)
        out = out.T
        osend[i] = jnp.where(
            low_half(HALF), pltpu.roll(out[:HALF], 64, 1), out[HALF:]
        ).astype(BF16)

        @pl.when(me != 4 + i)
        def _():
            o_copy(i).start()

        @pl.when(me == 4 + i)
        def _():
            o_own(i).start()

    def collect(buf, recv, own, start, masked):
        for h in range(8):
            @pl.when(me == h)
            def _():
                own(quad).wait()

            @pl.when(me != h)
            def _():
                remote(buf.at[h], buf.at[h], recv.at[h], recv.at[h], peer(h)).wait_recv()
        for g in range(4):
            a, b = exchange(buf[2 * g].astype(F32), buf[2 * g + 1].astype(F32))
            pair = jnp.concatenate([a, b], 0)
            if masked:
                pair = jnp.where(row_live, pair, 0.0)
            left[:, start + g * 128:start + (g + 1) * 128] = pair.astype(BF16)

    def piece(columns, y, part, with_rows):
        @pl.loop(0, 4)
        def _(j):
            rows = pl.ds(pl.multiple_of(y * SLICE + j * 256, 256), 256)
            value = lax.dot_general(
                left[:, columns], wcat[rows, columns], NT, preferred_element_type=F32
            ).astype(BF16)
            part[y, :, pl.ds(pl.multiple_of(j * 256, 256), 256)] = value
            if with_rows:
                term = value.astype(F32) * (states[:, rows].astype(F32) * gains[:, rows])
                rterm[...] += term[:, :128] + term[:, 128:]

    def rs_copy(n, part, far, into, send, recv):
        src, dst, y = [
            (part.at[y_far, top], far.at[0], y_r),
            (part.at[y_far, bottom], far.at[1], y_l),
            (part.at[y_r, bottom], into.at[0, bottom], y_r),
            (part.at[y_r, top], into.at[0, top], y_r),
            (part.at[y_l, top], into.at[1, top], y_l),
            (part.at[y_l, bottom], into.at[1, bottom], y_l),
        ][n]
        return remote(src, dst, send.at[n], recv.at[n], at_y(y))

    def rs_recv(n, part, far, into, send, recv):
        dst = [
            far.at[0], far.at[1], into.at[0, bottom], into.at[0, top],
            into.at[1, top], into.at[1, bottom],
        ][n]
        remote(dst, dst, send.at[n], recv.at[n], at_y(y_r)).wait_recv()

    def rs_begin(columns, with_rows, args):
        part = args[0]
        piece(columns, y_far, part, with_rows)
        rs_copy(0, *args).start()
        rs_copy(1, *args).start()
        piece(columns, y_r, part, with_rows)
        rs_copy(2, *args).start()
        piece(columns, y_l, part, with_rows)
        rs_copy(4, *args).start()
        piece(columns, mp, part, with_rows)

    def rs_middle(args):
        part, far = args[:2]
        rs_recv(0, *args)
        part[y_r, top] = (part[y_r, top].astype(F32) + far[0].astype(F32)).astype(BF16)
        rs_copy(3, *args).start()
        rs_recv(1, *args)
        part[y_l, bottom] = (part[y_l, bottom].astype(F32) + far[1].astype(F32)).astype(BF16)
        rs_copy(5, *args).start()

    def rs_wait(args):
        for n in (2, 4, 3, 5):
            rs_recv(n, *args)

    l_args = (lpart, lfar, lin, l_s, l_r)
    g_args = (gpart, gfar, gin, rs_s, rs_r)
    first, second = pl.ds(0, GROUP), pl.ds(GROUP, GROUP)

    @pl.when(seg == 1)
    def _():
        for n in (1, 3, 4, 5):
            cot_recv(n)
        acc[:, GROUP:] = jnp.zeros((ROWS, GROUP), F32)

        @pl.loop(0, 4)
        def _(c):
            rows = pl.ds(pl.multiple_of(c * SLICE, SLICE), SLICE)
            acc[:, GROUP:] += jnp.dot(cot[c], wcat[rows, GROUP:], preferred_element_type=F32)

        for g in range(4):
            pair = jnp.where(row_live, acc[:, GROUP + g * 128:GROUP + (g + 1) * 128], 0.0)
            even, odd = exchange(pair[:HALF], pair[HALF:])
            dsend[2 * g] = even.astype(BF16)
            dsend[2 * g + 1] = odd.astype(BF16)
        for k in range(1, 8):
            d_copy(lax.rem(me + k, 8)).start()
        d_own.start()
        collect(obuf, o_r, o_own, GROUP, True)
        rs_begin(second, False, l_args)

    gacc[...] = jnp.zeros_like(gacc)

    def zg_copy(s):
        return remote(zout.at[s], zin.at[s], zg_s.at[s], zg_r.at[s], at_z(z_dn))

    @pl.loop(0, 4)
    def _(i):
        from_summary(dbuf, d_r, d_own, i)
        q0 = query(i)
        d0 = gradient(i)
        qd = q0 + d0
        delta = jnp.zeros((1, ROWS), F32)
        for j in range(4):
            dp = lax.dot_general(docs[i + j, :ROWS], d0, NT, preferred_element_type=F32)
            dpbuf[j] = dp
            delta = delta + jnp.sum(sbuf[i, j] * dp, axis=0, keepdims=True)
        out = jnp.zeros((128, ROWS), F32)
        low = low_half(ROWS)
        for j in range(4):
            ds = (sbuf[i, j] * (dpbuf[j] - delta)).astype(BF16)
            out = out + lax.dot_general(docs[i + j, :ROWS], ds, TN, preferred_element_type=F32)
            gk = jnp.dot(ds, qd, preferred_element_type=F32)
            gv = jnp.dot(pbuf[i, j], qd, preferred_element_type=F32)
            gacc[i + j] += jnp.where(low, SCALE * gk, gv)
        out = (SCALE * out).T
        dqsend[i] = jnp.where(
            low_half(HALF), out[:HALF], pltpu.roll(out[HALF:], 64, 1)
        ).astype(BF16)

        @pl.when(me != 4 + i)
        def _():
            dq_copy(i).start()

        @pl.when(me == 4 + i)
        def _():
            dq_own(i).start()

        @pl.when(i < 3)
        def _():
            zout[i] = gacc[i].astype(BF16)
            zg_copy(i).start()

    def g_copy(j):
        return remote(gout.at[j], gbuf.at[me], g_s.at[j], g_r.at[me], peer(j))

    def g_own(j):
        return pltpu.make_async_copy(gout.at[j], gbuf.at[me], loc_sem.at[2])

    for j in range(4):
        total = gacc[3 + j]
        if j > 0:
            remote(zin.at[j - 1], zin.at[j - 1], zg_s.at[0], zg_r.at[j - 1], at_z(z_up)).wait_recv()
            total = total + zin[j - 1].astype(F32)
        gout[j] = total.astype(BF16)

        @pl.when(me != j)
        def _():
            g_copy(j).start()

        @pl.when(me == j)
        def _():
            g_own(j).start()

    rterm[...] = jnp.zeros_like(rterm)

    @pl.when(seg == 1)
    def _():
        rs_middle(l_args)
        collect(dqbuf, dq_r, dq_own, 0, False)
        rs_begin(first, True, g_args)

    @pl.when(seg == 0)
    def _():
        for h in range(8):
            @pl.when(me == h)
            def _():
                g_own(quad).wait()

            @pl.when(me != h)
            def _():
                remote(gbuf.at[h], gbuf.at[h], g_r.at[h], g_r.at[h], peer(h)).wait_recv()
        for g in range(4):
            a, b = exchange(gbuf[2 * g].astype(F32), gbuf[2 * g + 1].astype(F32))
            left[:, g * 128:(g + 1) * 128] = a.astype(BF16)
            left[:, GROUP + g * 128:GROUP + (g + 1) * 128] = b.astype(BF16)
        rs_begin(pl.ds(0, 2 * GROUP), True, g_args)

    rsend[...] = jnp.broadcast_to(jnp.sum(rterm[...].T, axis=0, keepdims=True), (8, ROWS))

    def rt_copy(n, y):
        return remote(rsend, rin.at[n], rt_s.at[n], rt_r.at[n], at_y(y))

    for n, y in enumerate((y_r, y_l, y_far)):
        rt_copy(n, y).start()

    rs_middle(g_args)

    layer_out = pltpu.make_async_copy(lout, seg_hbm.at[0], out_sem.at[0])

    @pl.when(seg == 1)
    def _():
        rs_wait(l_args)

        @pl.loop(0, 8)
        def _(i):
            rows = pl.ds(pl.multiple_of(i * 32, 32), 32)
            value = lpart[mp, rows].astype(F32) + lin[0, rows].astype(F32) + lin[1, rows].astype(F32)
            lout[rows] = value.astype(BF16)

        layer_out.start()

    for n in range(3):
        remote(rin.at[n], rin.at[n], rt_s.at[n], rt_r.at[n], at_y(y_r)).wait_recv()
    sums = (rsend[...] + rin[0]) + (rin[1] + rin[2])
    rterm[...] = jnp.broadcast_to(sums[:1], (128, ROWS)).T

    rs_wait(g_args)

    @pl.loop(0, 8)
    def _(i):
        rows = pl.ds(pl.multiple_of(i * 32, 32), 32)
        value = gpart[mp, rows].astype(F32) + gin[0, rows].astype(F32) + gin[1, rows].astype(F32)
        inverse = rspread[rows]
        factor = rterm[rows] * (inverse * inverse * inverse) * (1.0 / WIDTH)
        gain = gains[:, own_columns]
        x = states[rows, own_columns].astype(F32)
        gfin[rows] = (gain * value * inverse[:, :1] - x * factor[:, :1]).astype(BF16)

    grad_out = pltpu.make_async_copy(gfin, grad_hbm.at[0], out_sem.at[1])
    grad_out.start()

    @pl.when(seg == 0)
    def _():
        normed_out.wait()
        for k in range(1, 8):
            kv_copy(lax.rem(me + k, 8)).wait_send()

    @pl.when(seg == 1)
    def _():
        layer_out.wait()
        for n in range(6):
            cot_copy(n).wait_send()
            rs_copy(n, *l_args).wait_send()
        for k in range(1, 8):
            q_copy(lax.rem(me + k, 8)).wait_send()
            d_copy(lax.rem(me + k, 8)).wait_send()

    for s in range(3):
        z_copy(s).wait_send()
        zg_copy(s).wait_send()
    for i in range(4):
        @pl.when(me != 4 + i)
        def _():
            o_copy(i).wait_send()
            dq_copy(i).wait_send()

        @pl.when(me != i)
        def _():
            g_copy(i).wait_send()
    for n in range(6):
        rs_copy(n, *g_args).wait_send()
    for n, y in enumerate((y_r, y_l, y_far)):
        rt_copy(n, y).wait_send()
    grad_out.wait()


def per_device(segment_in, norm_gains, projections, live_counts, cotangent):
    dma = lambda n: pltpu.SemaphoreType.DMA((n,))
    vmem = pltpu.VMEM
    shape = jax.ShapeDtypeStruct((1, ROWS, SLICE), BF16)
    hbm = pl.BlockSpec(memory_space=pl.ANY)
    return pl.pallas_call(
        kernel,
        name="window_attention",
        out_shape=(shape, shape),
        in_specs=[pl.BlockSpec(memory_space=pltpu.SMEM)] + [hbm] * 4,
        out_specs=(hbm, hbm),
        scratch_shapes=[
            vmem((ROWS, WIDTH), BF16),
            vmem((1, WIDTH), F32),
            vmem((ROWS, WIDTH), BF16),
            vmem((ROWS, 128), F32),
            vmem((WIDTH, 2, GROUP), BF16),
            vmem((WIDTH, 2 * GROUP), BF16),
            vmem((ROWS, 2 * GROUP), F32),
            vmem((4, ROWS, SLICE), BF16),
            vmem((8, SLAB, 128), BF16),
            vmem((8, HALF, 128), BF16),
            vmem((8, HALF, 128), BF16),
            vmem((7, SLAB, 128), BF16),
            vmem((4, HALF, 128), BF16),
            vmem((4, HALF, 128), BF16),
            vmem((4, 4, ROWS, ROWS), F32),
            vmem((4, 4, ROWS, ROWS), BF16),
            vmem((4, ROWS, ROWS), F32),
            vmem((7, ROWS, 128), F32),
            vmem((4, HALF, 128), BF16),
            vmem((4, HALF, 128), BF16),
            vmem((8, HALF, 128), BF16),
            vmem((8, HALF, 128), BF16),
            vmem((3, ROWS, 128), BF16),
            vmem((3, ROWS, 128), BF16),
            vmem((4, ROWS, 128), BF16),
            vmem((8, ROWS, 128), BF16),
            vmem((ROWS, 2 * GROUP), BF16),
            vmem((4, ROWS, SLICE), BF16),
            vmem((2, HALF, SLICE), BF16),
            vmem((2, ROWS, SLICE), BF16),
            vmem((4, ROWS, SLICE), BF16),
            vmem((2, HALF, SLICE), BF16),
            vmem((2, ROWS, SLICE), BF16),
            vmem((ROWS, 128), F32),
            vmem((8, ROWS), F32),
            vmem((3, 8, ROWS), F32),
            vmem((ROWS, SLICE), BF16),
            vmem((ROWS, SLICE), BF16),
            dma(3), dma(4), dma(4), dma(2),
            dma(6), dma(6), dma(8), dma(7), dma(8), dma(4), dma(8), dma(4), dma(3), dma(3),
            dma(4), dma(8), dma(4), dma(8), dma(3), dma(3), dma(4), dma(8),
            dma(6), dma(6), dma(6), dma(6), dma(3), dma(3),
        ],
        compiler_params=pltpu.CompilerParams(
            collective_id=0, has_side_effects=True, vmem_limit_bytes=56 * 1024 * 1024
        ),
        cost_estimate=pl.CostEstimate(flops=10**10, bytes_accessed=12 * 2**20, transcendentals=2**20),
    )(live_counts, segment_in, norm_gains, projections, cotangent)


def solution(mesh):
    in_specs = (
        P("segment", "blk", None),
        P("segment", None),
        P("segment", None, None, "mp"),
        P(None, "blk"),
        P("blk", "mp"),
    )
    out_specs = (P("segment", "blk", "mp"), P("segment", "blk", "mp"))
    return jax.shard_map(
        per_device, mesh=mesh, in_specs=in_specs, out_specs=out_specs, check_vma=False
    )
```

time: 252 us -> 82.5 us (0.33)
  Pallas kernels: 0 us -> 76.2 us
  waiting for transfers between devices: 62.9 us -> 0 us
  local copies, waits for them, and re-layouts: 51.3 us -> 5.03 us
  starting transfers between devices: 43.4 us -> 0 us
  matrix products: 40.7 us -> 0 us
  other arithmetic: 29.7 us -> 0 us
  between operations: 14.2 us -> 0.64 us
  blocking collectives: 8.58 us -> 0 us
    pallas_call x0 -> x1, Pallas kernels: none -> 76.2 us  [per_device(): pl.pallas_call(kernel, name='window_attention', out_shape=(shape, shape),...]
    reduce_scatter x2 -> x0, waiting for transfers between devices: 45.4 us -> none  [the longest x1 45.4 us: per_device(): lax.psum_scatter(partial_grad.astype(jnp.bfloat16), 'mp', scatter_dimensi...]
    ppermute x19 -> x0, starting transfers between devices: 43.3 us -> none  [from_behind(): return lax.ppermute(x, axis, pairs)]
    dot_general x9 -> x0, matrix products: 33.3 us -> none  [the longest x2 7.59 us: right_product(): lax.dot_general(left, right, (((1,), (1,)), ((), ())), preferred_element_...]
    slice x6 -> x0, local copies, waits for them, and re-layouts: 22 us -> none  [the longest x1 17.6 us: per_device(): w_primary = projections[0, :, 0, :]]
    ppermute x19 -> x0, waiting for transfers between devices: 17.4 us -> none  [from_behind(): return lax.ppermute(x, axis, pairs)]
    convert_element_type x9 -> x0, other arithmetic: 14.2 us -> none  [the longest x2 3.62 us: per_device(): value_total.astype(jnp.bfloat16)]
    squeeze x6 -> x0, local copies, waits for them, and re-layouts: 9.71 us -> none  [the longest x3 5.31 us: per_device(): value_total = arrived[1] + value_parts[offset]]
  transfers between devices with their start and end apart: 22 -> 0, of which waited for: 5 -> 0; matrix products, arithmetic and copies ran while one was open for 34% -> 0% of each run, Pallas kernels for 0% -> 0%
where the time goes in v1:
time: 82.5 us; the launch traced here: 81.9 us
  Pallas kernels  76.2 us (92%)
  local copies, waits for them, and re-layouts  5.03 us (6%)
    pallas_call x1, Pallas kernels, per_device(): pl.pallas_call(kernel, name='window_attention', out_shape=(shape, shape),...  76.2 us
    unnamed x3, local copies, waits for them, and re-layouts  5.03 us

profile of v1, /device:TPU:2, one launch (start us, length us, event | category | flops | bytes accessed | tf_op | source)
XLA Modules:
  0.0 81.9 jit_solution(13706693928952959815)
XLA Ops:
  0.6 1.3 %copy.7.live_ref = s32[2,1]{1,0:T(2,128)} copy(s32[2,1]{0,1:T(1,128)} %param.8) | data formatting | bytes 16 | tf_op args[3]
  1.9 76.2 %window_attention.1 = (bf16[1,256,1024]{2,1,0:T(8,128)(2,1)}, bf16[1,256,1024]{2,1,0:T(8,128)(2,1)}) custom-call(s32[2,1]{1,0:T(2,128)} %copy.7.live_ref, bf16[1,256,4096]{2,1,0:T(8,128)(2,1)} %x_hbm.1, f32[1,4096]{1,0:T(1,128)} %gain_hbm.1, bf16[1,4096,2,512]{3,2,1,0:T(2,128)(2,1)} %w_hbm.1, bf16[256,1024]{1,0:T(8,128)(2,1)} %cot_hbm.1), custom_call_target="tpu_custom_call" | custom-call | flops 10000000000 | bytes 12582912 | tf_op jit(solution)/shard_map/window_attention/pallas_call | solution.py:571
  78.2 1.9 %copy.10 = bf16[1,256,1024]{2,1,0:T(8,128)(2,1)} copy(bf16[1,256,1024]{2,1,0:T(8,128)(2,1)} %get-tuple-element.4) | data formatting | bytes 1048576
  80.0 1.9 %copy.11 = bf16[1,256,1024]{2,1,0:T(8,128)(2,1)} copy(bf16[1,256,1024]{2,1,0:T(8,128)(2,1)} %get-tuple-element.5) | data formatting | bytes 1048576

commit v2 on v1

--- a/solution.py
+++ b/solution.py
@@ -83,7 +83,6 @@
         pl.semaphore_signal(barrier, inc=1, device_id=peer(lax.rem(me + k, 8)), device_id_type=MESH)
     for to in (at_y(y_r), at_y(y_l), at_y(y_far), at_z(z_up), at_z(z_dn)):
         pl.semaphore_signal(barrier, inc=1, device_id=to, device_id_type=MESH)
-    pl.semaphore_wait(barrier, 12)
 
     top, bottom = pl.ds(0, HALF), pl.ds(HALF, HALF)
 
@@ -103,23 +102,26 @@
         ][n]
         remote(ref, ref, cot_s.at[n], cot_r.at[n], at_y(y_r)).wait_recv()
 
-    @pl.when(seg == 1)
-    def _():
-        c_load.wait()
-        for n in (0, 2, 1, 3):
-            cot_copy(n).start()
-
-    x_load.wait()
-    g_load.wait()
-
-    @pl.loop(0, 8)
-    def _(i):
+    def norm(i):
         rows = pl.ds(pl.multiple_of(i * 32, 32), 32)
         x = states[rows].astype(F32)
         inverse = 1.0 / jnp.sqrt(jnp.mean(x * x, axis=-1, keepdims=True) + EPSILON)
         rspread[rows] = jnp.broadcast_to(inverse, (32, 128))
         normed[rows] = (x * inverse * gains[...]).astype(BF16)
 
+    x_load.wait()
+    g_load.wait()
+    pl.loop(0, 4)(norm)
+    pl.semaphore_wait(barrier, 12)
+
+    @pl.when(seg == 1)
+    def _():
+        c_load.wait()
+        for n in (0, 2, 1, 3):
+            cot_copy(n).start()
+
+    pl.loop(4, 8)(norm)
+
     own_columns = pl.ds(pl.multiple_of(mp * SLICE, SLICE), SLICE)
     normed_out = pltpu.make_async_copy(normed.at[:, own_columns], seg_hbm.at[0], out_sem.at[0])
 
@@ -127,68 +129,76 @@
     def _():
         normed_out.start()
 
-    acc[...] = jnp.zeros_like(acc)
-
-    @pl.loop(0, 4)
-    def _(c):
-        w_load(c).wait()
+    def low_half(rows):
+        return lax.broadcasted_iota(jnp.int32, (rows, 128), 1) < 64
+
+    def exchange(a, b):
+        low = low_half(a.shape[0])
+        return jnp.where(low, a, pltpu.roll(b, 64, 1)), jnp.where(low, pltpu.roll(a, 64, 1), b)
+
+    row_live = lax.broadcasted_iota(jnp.int32, (ROWS, 128), 0) < live_ref[0, 1]
+
+    def kv_copy(t):
+        return remote(kvsend.at[t], docs.at[3 + quad], kv_s.at[t], doc_r.at[3 + quad], peer(t))
+
+    def q_copy(t):
+        return remote(qsend.at[t], qbuf.at[quad], q_s.at[t], q_r.at[quad], peer(t))
+
+    def d_copy(t):
+        return remote(dsend.at[t], dbuf.at[quad], d_s.at[t], d_r.at[quad], peer(t))
+
+    kv_own = pltpu.make_async_copy(kvsend.at[me], docs.at[3 + quad], loc_sem.at[0])
+    q_own = pltpu.make_async_copy(qsend.at[me], qbuf.at[quad], loc_sem.at[0])
+    d_own = pltpu.make_async_copy(dsend.at[me], dbuf.at[quad], loc_sem.at[1])
+
+    @pl.when(seg == 0)
+    def _():
+        for c in range(4):
+            w_load(c).wait()
+        count = jnp.full((16, 128), live_ref[0, 0], jnp.int32).astype(F32).astype(BF16)
+        chip = quad // 2
+        for pair in (2 + chip, 3 - chip, 1 - chip, chip):
+            source = pl.ds(pl.multiple_of(pair * 128, 128), 128)
+            columns = pl.ds(pl.multiple_of(pair * 256, 256), 256)
+
+            @pl.loop(0, 16)
+            def _(j):
+                rows = pl.ds(pl.multiple_of(j * 256, 256), 256)
+                wcat[rows, columns] = wraw[rows, :, source].reshape(256, 256)
+
+            both = jnp.dot(normed[...], wcat[:, columns], preferred_element_type=F32)
+            even, odd = exchange(both[:, :128], both[:, 128:])
+            for k, slab in enumerate((even, odd)):
+                t = 2 * pair + k
+                kvsend[t, :ROWS] = slab.astype(BF16)
+                kvsend[t, ROWS:] = count
+
+                @pl.when(t != me)
+                def _():
+                    kv_copy(t).start()
+
+                @pl.when(t == me)
+                def _():
+                    kv_own.start()
+
+    @pl.when(seg == 1)
+    def _():
+        acc[...] = jnp.zeros_like(acc)
 
         @pl.loop(0, 4)
-        def _(j):
-            rows = pl.ds(pl.multiple_of(c * SLICE + j * 256, 256), 256)
-            wcat[rows] = wraw[rows].reshape(256, 2 * GROUP)
-
-        rows = pl.ds(pl.multiple_of(c * SLICE, SLICE), SLICE)
-
-        @pl.when(seg == 0)
-        def _():
-            acc[...] += jnp.dot(normed[:, rows], wcat[rows], preferred_element_type=F32)
-
-        @pl.when(seg == 1)
-        def _():
+        def _(c):
+            w_load(c).wait()
+
+            @pl.loop(0, 4)
+            def _(j):
+                rows = pl.ds(pl.multiple_of(c * SLICE + j * 256, 256), 256)
+                wcat[rows] = wraw[rows].reshape(256, 2 * GROUP)
+
+            rows = pl.ds(pl.multiple_of(c * SLICE, SLICE), SLICE)
             acc[:, :GROUP] += jnp.dot(
                 normed[:, rows], wcat[rows, :GROUP], preferred_element_type=F32
             )
 
-    def low_half(rows):
-        return lax.broadcasted_iota(jnp.int32, (rows, 128), 1) < 64
-
-    def exchange(a, b):
-        low = low_half(a.shape[0])
-        return jnp.where(low, a, pltpu.roll(b, 64, 1)), jnp.where(low, pltpu.roll(a, 64, 1), b)
-
-    row_live = lax.broadcasted_iota(jnp.int32, (ROWS, 128), 0) < live_ref[1, 0]
-
-    def kv_copy(t):
-        return remote(kvsend.at[t], docs.at[3 + quad], kv_s.at[t], doc_r.at[3 + quad], peer(t))
-
-    def q_copy(t):
-        return remote(qsend.at[t], qbuf.at[quad], q_s.at[t], q_r.at[quad], peer(t))
-
-    def d_copy(t):
-        return remote(dsend.at[t], dbuf.at[quad], d_s.at[t], d_r.at[quad], peer(t))
-
-    kv_own = pltpu.make_async_copy(kvsend.at[me], docs.at[3 + quad], loc_sem.at[0])
-    q_own = pltpu.make_async_copy(qsend.at[me], qbuf.at[quad], loc_sem.at[0])
-    d_own = pltpu.make_async_copy(dsend.at[me], dbuf.at[quad], loc_sem.at[1])
-
-    @pl.when(seg == 0)
-    def _():
-        count = jnp.full((16, 128), live_ref[0, 0], jnp.int32).astype(F32).astype(BF16)
-        for g in range(4):
-            keys = acc[:, g * 128:(g + 1) * 128]
-            values = acc[:, GROUP + g * 128:GROUP + (g + 1) * 128]
-            even, odd = exchange(keys, values)
-            kvsend[2 * g, :ROWS] = even.astype(BF16)
-            kvsend[2 * g + 1, :ROWS] = odd.astype(BF16)
-            kvsend[2 * g, ROWS:] = count
-            kvsend[2 * g + 1, ROWS:] = count
-        for k in range(1, 8):
-            kv_copy(lax.rem(me + k, 8)).start()
-        kv_own.start()
-
-    @pl.when(seg == 1)
-    def _():
         for g in range(4):
             pair = acc[:, g * 128:(g + 1) * 128]
             even, odd = exchange(pair[:HALF], pair[HALF:])
@@ -208,7 +218,7 @@
     def z_recv(s):
         remote(docs.at[s], docs.at[s], z_s.at[s], z_r.at[s], at_z(z_up)).wait_recv()
 
-    for j in (1, 2, 3, 0):
+    for j in (3, 2, 1, 0):
         @pl.when(me == j)
         def _():
             kv_own.wait()
@@ -377,14 +387,18 @@
 
     @pl.when(seg == 1)
     def _():
-        for n in (1, 3, 4, 5):
+        for n in (1, 3):
             cot_recv(n)
-        acc[:, GROUP:] = jnp.zeros((ROWS, GROUP), F32)
-
-        @pl.loop(0, 4)
-        def _(c):
+
+        def gather_product(k):
+            c = lax.rem(y_far + k, 4)
             rows = pl.ds(pl.multiple_of(c * SLICE, SLICE), SLICE)
             acc[:, GROUP:] += jnp.dot(cot[c], wcat[rows, GROUP:], preferred_element_type=F32)
+
+        pl.loop(1, 4)(gather_product)
+        for n in (4, 5):
+            cot_recv(n)
+        gather_product(0)
 
         for g in range(4):
             pair = jnp.where(row_live, acc[:, GROUP + g * 128:GROUP + (g + 1) * 128], 0.0)
@@ -480,8 +494,8 @@
                 remote(gbuf.at[h], gbuf.at[h], g_r.at[h], g_r.at[h], peer(h)).wait_recv()
         for g in range(4):
             a, b = exchange(gbuf[2 * g].astype(F32), gbuf[2 * g + 1].astype(F32))
-            left[:, g * 128:(g + 1) * 128] = a.astype(BF16)
-            left[:, GROUP + g * 128:GROUP + (g + 1) * 128] = b.astype(BF16)
+            left[:, g * 256:g * 256 + 128] = a.astype(BF16)
+            left[:, g * 256 + 128:(g + 1) * 256] = b.astype(BF16)
         rs_begin(pl.ds(0, 2 * GROUP), True, g_args)
 
     rsend[...] = jnp.broadcast_to(jnp.sum(rterm[...].T, axis=0, keepdims=True), (8, ROWS))
@@ -563,12 +577,23 @@
     grad_out.wait()
 
 
+def deliver(seg_in, grad_in, seg_out, grad_out, sem):
+    copies = [
+        pltpu.make_async_copy(seg_in, seg_out, sem.at[0]),
+        pltpu.make_async_copy(grad_in, grad_out, sem.at[1]),
+    ]
+    for copy in copies:
+        copy.start()
+    for copy in copies:
+        copy.wait()
+
+
 def per_device(segment_in, norm_gains, projections, live_counts, cotangent):
     dma = lambda n: pltpu.SemaphoreType.DMA((n,))
     vmem = pltpu.VMEM
     shape = jax.ShapeDtypeStruct((1, ROWS, SLICE), BF16)
     hbm = pl.BlockSpec(memory_space=pl.ANY)
-    return pl.pallas_call(
+    results = pl.pallas_call(
         kernel,
         name="window_attention",
         out_shape=(shape, shape),
@@ -622,7 +647,15 @@
             collective_id=0, has_side_effects=True, vmem_limit_bytes=56 * 1024 * 1024
         ),
         cost_estimate=pl.CostEstimate(flops=10**10, bytes_accessed=12 * 2**20, transcendentals=2**20),
-    )(live_counts, segment_in, norm_gains, projections, cotangent)
+    )(live_counts.reshape(1, 2), segment_in, norm_gains, projections, cotangent)
+    return pl.pallas_call(
+        deliver,
+        name="deliver",
+        out_shape=(shape, shape),
+        in_specs=[hbm] * 2,
+        out_specs=(hbm, hbm),
+        scratch_shapes=[dma(2)],
+    )(*results)
 
 
 def solution(mesh):

time: 82.5 us -> 109 us (1.32)
  Pallas kernels: 76.2 us -> 109 us
  local copies, waits for them, and re-layouts: 5.03 us -> 0 us
    pallas_call x0 -> x1, Pallas kernels: none -> 32.9 us  [per_device(): pl.pallas_call(deliver, name='deliver', out_shape=(shape, shape), in_spec...]
    unnamed x3 -> x0, local copies, waits for them, and re-layouts: 5.03 us -> none
where the time goes in v2:
time: 109 us
  Pallas kernels  109 us (100%)
    pallas_call x1, Pallas kernels, per_device(): pl.pallas_call(kernel, name='window_attention', out_shape=(shape, shape),...  75.8 us
    pallas_call x1, Pallas kernels, per_device(): pl.pallas_call(deliver, name='deliver', out_shape=(shape, shape), in_spec...  32.9 us

profile of v2, /device:TPU:2, one launch (start us, length us, event | category | flops | bytes accessed | tf_op | source)
XLA Modules:
  0.0 109.3 jit_solution(16726977687782921064)
XLA Ops:
  0.6 75.8 %window_attention.1 = (bf16[1,256,1024]{2,1,0:T(8,128)(2,1)}, bf16[1,256,1024]{2,1,0:T(8,128)(2,1)}) custom-call(s32[1,2]{1,0:T(1,128)} %bitcast.1, bf16[1,256,4096]{2,1,0:T(8,128)(2,1)} %x_hbm.1, f32[1,4096]{1,0:T(1,128)} %gain_hbm.1, bf16[1,4096,2,512]{3,2,1,0:T(2,128)(2,1)} %w_hbm.1, bf16[256,1024]{1,0:T(8,128)(2,1)} %cot_hbm.1), custom_call_target="tpu_custom_call" | custom-call | flops 10000000000 | bytes 12582912 | tf_op jit(solution)/shard_map/window_attention/pallas_call | solution.py:596
  76.4 32.9 %deliver.1 = (bf16[1,256,1024]{2,1,0:T(8,128)(2,1)}, bf16[1,256,1024]{2,1,0:T(8,128)(2,1)}) custom-call(bf16[1,256,1024]{2,1,0:T(8,128)(2,1)} %get-tuple-element.4.seg_in, bf16[1,256,1024]{2,1,0:T(8,128)(2,1)} %get-tuple-element.5.grad_in), custom_call_target="tpu_custom_call" | custom-call | tf_op jit(solution)/shard_map/deliver/pallas_call | solution.py:651

commit v3 on v2

--- a/solution.py
+++ b/solution.py
@@ -112,12 +112,12 @@
     x_load.wait()
     g_load.wait()
     pl.loop(0, 4)(norm)
-    pl.semaphore_wait(barrier, 12)
 
     @pl.when(seg == 1)
     def _():
+        pl.semaphore_wait(barrier, 12)
         c_load.wait()
-        for n in (0, 2, 1, 3):
+        for n in (0, 2):
             cot_copy(n).start()
 
     pl.loop(4, 8)(norm)
@@ -151,35 +151,36 @@
     q_own = pltpu.make_async_copy(qsend.at[me], qbuf.at[quad], loc_sem.at[0])
     d_own = pltpu.make_async_copy(dsend.at[me], dbuf.at[quad], loc_sem.at[1])
 
+    def spread_weights(c):
+        w_load(c).wait()
+
+        @pl.loop(0, 4)
+        def _(j):
+            rows = pl.ds(pl.multiple_of(c * SLICE + j * 256, 256), 256)
+            wcat[rows] = wraw[rows].reshape(256, 2 * GROUP)
+
     @pl.when(seg == 0)
     def _():
-        for c in range(4):
-            w_load(c).wait()
+        pl.loop(0, 4)(spread_weights)
+        pl.semaphore_wait(barrier, 12)
         count = jnp.full((16, 128), live_ref[0, 0], jnp.int32).astype(F32).astype(BF16)
-        chip = quad // 2
-        for pair in (2 + chip, 3 - chip, 1 - chip, chip):
-            source = pl.ds(pl.multiple_of(pair * 128, 128), 128)
-            columns = pl.ds(pl.multiple_of(pair * 256, 256), 256)
-
-            @pl.loop(0, 16)
-            def _(j):
-                rows = pl.ds(pl.multiple_of(j * 256, 256), 256)
-                wcat[rows, columns] = wraw[rows, :, source].reshape(256, 256)
-
-            both = jnp.dot(normed[...], wcat[:, columns], preferred_element_type=F32)
-            even, odd = exchange(both[:, :128], both[:, 128:])
-            for k, slab in enumerate((even, odd)):
-                t = 2 * pair + k
-                kvsend[t, :ROWS] = slab.astype(BF16)
-                kvsend[t, ROWS:] = count
-
-                @pl.when(t != me)
-                def _():
+        for stage in (1, 0):
+            start = stage * 256
+            keys = jnp.dot(normed[...], wcat[:, start:start + 256], preferred_element_type=F32)
+            start = GROUP + start
+            values = jnp.dot(normed[...], wcat[:, start:start + 256], preferred_element_type=F32)
+            for g in range(2):
+                part = slice(g * 128, (g + 1) * 128)
+                for k, slab in enumerate(exchange(keys[:, part], values[:, part])):
+                    t = 4 * stage + 2 * g + k
+                    kvsend[t, :ROWS] = slab.astype(BF16)
+                    kvsend[t, ROWS:] = count
+            for k in range(4):
+                t = 4 * stage + lax.rem(quad + k, 4)
+                if stage == 0 and k == 0:
+                    kv_own.start()
+                else:
                     kv_copy(t).start()
-
-                @pl.when(t == me)
-                def _():
-                    kv_own.start()
 
     @pl.when(seg == 1)
     def _():
@@ -187,13 +188,7 @@
 
         @pl.loop(0, 4)
         def _(c):
-            w_load(c).wait()
-
-            @pl.loop(0, 4)
-            def _(j):
-                rows = pl.ds(pl.multiple_of(c * SLICE + j * 256, 256), 256)
-                wcat[rows] = wraw[rows].reshape(256, 2 * GROUP)
-
+            spread_weights(c)
             rows = pl.ds(pl.multiple_of(c * SLICE, SLICE), SLICE)
             acc[:, :GROUP] += jnp.dot(
                 normed[:, rows], wcat[rows, :GROUP], preferred_element_type=F32
@@ -208,9 +203,9 @@
             q_copy(lax.rem(me + k, 8)).start()
         q_own.start()
         cot_recv(0)
-        cot_copy(4).start()
         cot_recv(2)
-        cot_copy(5).start()
+        for n in (1, 3, 4, 5):
+            cot_copy(n).start()
 
     def z_copy(s):
         return remote(docs.at[s + 4], docs.at[s], z_s.at[s], z_r.at[s], at_z(z_up))
@@ -494,8 +489,8 @@
                 remote(gbuf.at[h], gbuf.at[h], g_r.at[h], g_r.at[h], peer(h)).wait_recv()
         for g in range(4):
             a, b = exchange(gbuf[2 * g].astype(F32), gbuf[2 * g + 1].astype(F32))
-            left[:, g * 256:g * 256 + 128] = a.astype(BF16)
-            left[:, g * 256 + 128:(g + 1) * 256] = b.astype(BF16)
+            left[:, g * 128:(g + 1) * 128] = a.astype(BF16)
+            left[:, GROUP + g * 128:GROUP + (g + 1) * 128] = b.astype(BF16)
         rs_begin(pl.ds(0, 2 * GROUP), True, g_args)
 
     rsend[...] = jnp.broadcast_to(jnp.sum(rterm[...].T, axis=0, keepdims=True), (8, ROWS))
@@ -577,15 +572,9 @@
     grad_out.wait()
 
 
-def deliver(seg_in, grad_in, seg_out, grad_out, sem):
-    copies = [
-        pltpu.make_async_copy(seg_in, seg_out, sem.at[0]),
-        pltpu.make_async_copy(grad_in, grad_out, sem.at[1]),
-    ]
-    for copy in copies:
-        copy.start()
-    for copy in copies:
-        copy.wait()
+def deliver(seg_in, grad_in, seg_out, grad_out):
+    seg_out[...] = seg_in[...]
+    grad_out[...] = grad_in[...]
 
 
 def per_device(segment_in, norm_gains, projections, live_counts, cotangent):
@@ -593,6 +582,7 @@
     vmem = pltpu.VMEM
     shape = jax.ShapeDtypeStruct((1, ROWS, SLICE), BF16)
     hbm = pl.BlockSpec(memory_space=pl.ANY)
+    half = pl.BlockSpec((1, HALF, SLICE), lambda i: (0, i, 0))
     results = pl.pallas_call(
         kernel,
         name="window_attention",
@@ -652,9 +642,9 @@
         deliver,
         name="deliver",
         out_shape=(shape, shape),
-        in_specs=[hbm] * 2,
-        out_specs=(hbm, hbm),
-        scratch_shapes=[dma(2)],
+        grid=(2,),
+        in_specs=[half] * 2,
+        out_specs=(half, half),
     )(*results)
 
 

time: 109 us -> 74.8 us (0.69)
  Pallas kernels: 109 us -> 74 us
    pallas_call x1, Pallas kernels: 32.9 us -> 2.04 us  [per_device(): pl.pallas_call(deliver, name='deliver', out_shape=(shape, shape), grid=(2...]
    pallas_call x1, Pallas kernels: 75.8 us -> 72 us  [per_device(): pl.pallas_call(kernel, name='window_attention', out_shape=(shape, shape),...]
where the time goes in v3:
time: 74.8 us; the launch traced here: 74.7 us
  Pallas kernels  74 us (99%)
    pallas_call x1, Pallas kernels, per_device(): pl.pallas_call(kernel, name='window_attention', out_shape=(shape, shape),...  72 us
    pallas_call x1, Pallas kernels, per_device(): pl.pallas_call(deliver, name='deliver', out_shape=(shape, shape), grid=(2...  2.04 us

profile of v3, /device:TPU:2, one launch (start us, length us, event | category | flops | bytes accessed | tf_op | source)
XLA Modules:
  0.0 74.7 jit_solution(6357557253338466888)
XLA Ops:
  0.6 72.0 %window_attention.1 = (bf16[1,256,1024]{2,1,0:T(8,128)(2,1)}, bf16[1,256,1024]{2,1,0:T(8,128)(2,1)}) custom-call(s32[1,2]{1,0:T(1,128)} %bitcast.1, bf16[1,256,4096]{2,1,0:T(8,128)(2,1)} %x_hbm.1, f32[1,4096]{1,0:T(1,128)} %gain_hbm.1, bf16[1,4096,2,512]{3,2,1,0:T(2,128)(2,1)} %w_hbm.1, bf16[256,1024]{1,0:T(8,128)(2,1)} %cot_hbm.1), custom_call_target="tpu_custom_call" | custom-call | flops 10000000000 | bytes 12582912 | tf_op jit(solution)/shard_map/window_attention/pallas_call | solution.py:586
  72.6 2.0 %deliver.1 = (bf16[1,256,1024]{2,1,0:T(8,128)(2,1)}, bf16[1,256,1024]{2,1,0:T(8,128)(2,1)}) custom-call(bf16[1,256,1024]{2,1,0:T(8,128)(2,1)} %get-tuple-element.4.seg_in, bf16[1,256,1024]{2,1,0:T(8,128)(2,1)} %get-tuple-element.5.grad_in), custom_call_target="tpu_custom_call" | custom-call | tf_op jit(solution)/shard_map/deliver/pallas_call | solution.py:641

commit v4 on v3

--- a/solution.py
+++ b/solution.py
@@ -322,17 +322,19 @@
                 pair = jnp.where(row_live, pair, 0.0)
             left[:, start + g * 128:start + (g + 1) * 128] = pair.astype(BF16)
 
-    def piece(columns, y, part, with_rows):
+    def piece(columns, y, part):
+        rows = pl.ds(pl.multiple_of(y * SLICE, SLICE), SLICE)
+        part[y] = lax.dot_general(
+            left[:, columns], wcat[rows, columns], NT, preferred_element_type=F32
+        ).astype(BF16)
+
+    def row_terms(y, part):
         @pl.loop(0, 4)
         def _(j):
             rows = pl.ds(pl.multiple_of(y * SLICE + j * 256, 256), 256)
-            value = lax.dot_general(
-                left[:, columns], wcat[rows, columns], NT, preferred_element_type=F32
-            ).astype(BF16)
-            part[y, :, pl.ds(pl.multiple_of(j * 256, 256), 256)] = value
-            if with_rows:
-                term = value.astype(F32) * (states[:, rows].astype(F32) * gains[:, rows])
-                rterm[...] += term[:, :128] + term[:, 128:]
+            value = part[y, :, pl.ds(pl.multiple_of(j * 256, 256), 256)]
+            term = value.astype(F32) * (states[:, rows].astype(F32) * gains[:, rows])
+            rterm[...] += term[:, :128] + term[:, 128:]
 
     def rs_copy(n, part, far, into, send, recv):
         src, dst, y = [
@@ -354,14 +356,17 @@
 
     def rs_begin(columns, with_rows, args):
         part = args[0]
-        piece(columns, y_far, part, with_rows)
+        piece(columns, y_far, part)
         rs_copy(0, *args).start()
         rs_copy(1, *args).start()
-        piece(columns, y_r, part, with_rows)
+        piece(columns, y_r, part)
         rs_copy(2, *args).start()
-        piece(columns, y_l, part, with_rows)
+        piece(columns, y_l, part)
         rs_copy(4, *args).start()
-        piece(columns, mp, part, with_rows)
+        piece(columns, mp, part)
+        if with_rows:
+            for y in (y_far, y_r, y_l, mp):
+                row_terms(y, part)
 
     def rs_middle(args):
         part, far = args[:2]
@@ -411,21 +416,22 @@
     def zg_copy(s):
         return remote(zout.at[s], zin.at[s], zg_s.at[s], zg_r.at[s], at_z(z_dn))
 
-    @pl.loop(0, 4)
-    def _(i):
+    for i in range(4):
         from_summary(dbuf, d_r, d_own, i)
+
+    for i in range(4):
         q0 = query(i)
         d0 = gradient(i)
         qd = q0 + d0
         delta = jnp.zeros((1, ROWS), F32)
         for j in range(4):
             dp = lax.dot_general(docs[i + j, :ROWS], d0, NT, preferred_element_type=F32)
-            dpbuf[j] = dp
+            dpbuf[i % 2, j] = dp
             delta = delta + jnp.sum(sbuf[i, j] * dp, axis=0, keepdims=True)
         out = jnp.zeros((128, ROWS), F32)
         low = low_half(ROWS)
         for j in range(4):
-            ds = (sbuf[i, j] * (dpbuf[j] - delta)).astype(BF16)
+            ds = (sbuf[i, j] * (dpbuf[i % 2, j] - delta)).astype(BF16)
             out = out + lax.dot_general(docs[i + j, :ROWS], ds, TN, preferred_element_type=F32)
             gk = jnp.dot(ds, qd, preferred_element_type=F32)
             gv = jnp.dot(pbuf[i, j], qd, preferred_element_type=F32)
@@ -434,19 +440,18 @@
         dqsend[i] = jnp.where(
             low_half(HALF), out[:HALF], pltpu.roll(out[HALF:], 64, 1)
         ).astype(BF16)
-
-        @pl.when(me != 4 + i)
-        def _():
-            dq_copy(i).start()
-
-        @pl.when(me == 4 + i)
-        def _():
-            dq_own(i).start()
-
-        @pl.when(i < 3)
-        def _():
+        if i < 3:
             zout[i] = gacc[i].astype(BF16)
             zg_copy(i).start()
+
+    for i in range(4):
+        @pl.when(me != 4 + i)
+        def _():
+            dq_copy(i).start()
+
+        @pl.when(me == 4 + i)
+        def _():
+            dq_own(i).start()
 
     def g_copy(j):
         return remote(gout.at[j], gbuf.at[me], g_s.at[j], g_r.at[me], peer(j))
@@ -606,7 +611,7 @@
             vmem((4, HALF, 128), BF16),
             vmem((4, 4, ROWS, ROWS), F32),
             vmem((4, 4, ROWS, ROWS), BF16),
-            vmem((4, ROWS, ROWS), F32),
+            vmem((2, 4, ROWS, ROWS), F32),
             vmem((7, ROWS, 128), F32),
             vmem((4, HALF, 128), BF16),
             vmem((4, HALF, 128), BF16),

time: 74.8 us -> 74.1 us (level)
  no operation moved by 1% of the time
where the time goes in v4:
time: 74.1 us; the launch traced here: 74 us
  Pallas kernels  73.3 us (99%)
    pallas_call x1, Pallas kernels, per_device(): pl.pallas_call(kernel, name='window_attention', out_shape=(shape, shape),...  71.3 us
    pallas_call x1, Pallas kernels, per_device(): pl.pallas_call(deliver, name='deliver', out_shape=(shape, shape), grid=(2...  2.04 us

profile of v4, /device:TPU:2, one launch (start us, length us, event | category | flops | bytes accessed | tf_op | source)
XLA Modules:
  0.0 74.0 jit_solution(14302571561153464880)
XLA Ops:
  0.6 71.3 %window_attention.1 = (bf16[1,256,1024]{2,1,0:T(8,128)(2,1)}, bf16[1,256,1024]{2,1,0:T(8,128)(2,1)}) custom-call(s32[1,2]{1,0:T(1,128)} %bitcast.1, bf16[1,256,4096]{2,1,0:T(8,128)(2,1)} %x_hbm.1, f32[1,4096]{1,0:T(1,128)} %gain_hbm.1, bf16[1,4096,2,512]{3,2,1,0:T(2,128)(2,1)} %w_hbm.1, bf16[256,1024]{1,0:T(8,128)(2,1)} %cot_hbm.1), custom_call_target="tpu_custom_call" | custom-call | flops 10000000000 | bytes 12582912 | tf_op jit(solution)/shard_map/window_attention/pallas_call | solution.py:591
  71.9 2.0 %deliver.1 = (bf16[1,256,1024]{2,1,0:T(8,128)(2,1)}, bf16[1,256,1024]{2,1,0:T(8,128)(2,1)}) custom-call(bf16[1,256,1024]{2,1,0:T(8,128)(2,1)} %get-tuple-element.4.seg_in, bf16[1,256,1024]{2,1,0:T(8,128)(2,1)} %get-tuple-element.5.grad_in), custom_call_target="tpu_custom_call" | custom-call | tf_op jit(solution)/shard_map/deliver/pallas_call | solution.py:646

commit v5 on v4

--- a/solution.py
+++ b/solution.py
@@ -206,6 +206,9 @@
         cot_recv(2)
         for n in (1, 3, 4, 5):
             cot_copy(n).start()
+
+    gacc[...] = jnp.zeros_like(gacc)
+    rterm[...] = jnp.zeros_like(rterm)
 
     def z_copy(s):
         return remote(docs.at[s + 4], docs.at[s], z_s.at[s], z_r.at[s], at_z(z_up))
@@ -411,7 +414,6 @@
         collect(obuf, o_r, o_own, GROUP, True)
         rs_begin(second, False, l_args)
 
-    gacc[...] = jnp.zeros_like(gacc)
 
     def zg_copy(s):
         return remote(zout.at[s], zin.at[s], zg_s.at[s], zg_r.at[s], at_z(z_dn))
@@ -444,15 +446,6 @@
             zout[i] = gacc[i].astype(BF16)
             zg_copy(i).start()
 
-    for i in range(4):
-        @pl.when(me != 4 + i)
-        def _():
-            dq_copy(i).start()
-
-        @pl.when(me == 4 + i)
-        def _():
-            dq_own(i).start()
-
     def g_copy(j):
         return remote(gout.at[j], gbuf.at[me], g_s.at[j], g_r.at[me], peer(j))
 
@@ -460,6 +453,16 @@
         return pltpu.make_async_copy(gout.at[j], gbuf.at[me], loc_sem.at[2])
 
     for j in range(4):
+        if j == 1:
+            for i in range(4):
+                @pl.when(me != 4 + i)
+                def _():
+                    dq_copy(i).start()
+
+                @pl.when(me == 4 + i)
+                def _():
+                    dq_own(i).start()
+
         total = gacc[3 + j]
         if j > 0:
             remote(zin.at[j - 1], zin.at[j - 1], zg_s.at[0], zg_r.at[j - 1], at_z(z_up)).wait_recv()
@@ -474,7 +477,6 @@
         def _():
             g_own(j).start()
 
-    rterm[...] = jnp.zeros_like(rterm)
 
     @pl.when(seg == 1)
     def _():

time: 74.1 us -> 74.1 us (level)
  no operation moved by 1% of the time
where the time goes in v5:
time: 74.1 us; the launch traced here: 74 us
  Pallas kernels  73.3 us (99%)
    pallas_call x1, Pallas kernels, per_device(): pl.pallas_call(kernel, name='window_attention', out_shape=(shape, shape),...  71.3 us
    pallas_call x1, Pallas kernels, per_device(): pl.pallas_call(deliver, name='deliver', out_shape=(shape, shape), grid=(2...  2.04 us

profile of v5, /device:TPU:2, one launch (start us, length us, event | category | flops | bytes accessed | tf_op | source)
XLA Modules:
  0.0 74.0 jit_solution(9723509058645769528)
XLA Ops:
  0.6 71.3 %window_attention.1 = (bf16[1,256,1024]{2,1,0:T(8,128)(2,1)}, bf16[1,256,1024]{2,1,0:T(8,128)(2,1)}) custom-call(s32[1,2]{1,0:T(1,128)} %bitcast.1, bf16[1,256,4096]{2,1,0:T(8,128)(2,1)} %x_hbm.1, f32[1,4096]{1,0:T(1,128)} %gain_hbm.1, bf16[1,4096,2,512]{3,2,1,0:T(2,128)(2,1)} %w_hbm.1, bf16[256,1024]{1,0:T(8,128)(2,1)} %cot_hbm.1), custom_call_target="tpu_custom_call" | custom-call | flops 10000000000 | bytes 12582912 | tf_op jit(solution)/shard_map/window_attention/pallas_call | solution.py:593
  71.9 2.0 %deliver.1 = (bf16[1,256,1024]{2,1,0:T(8,128)(2,1)}, bf16[1,256,1024]{2,1,0:T(8,128)(2,1)}) custom-call(bf16[1,256,1024]{2,1,0:T(8,128)(2,1)} %get-tuple-element.4.seg_in, bf16[1,256,1024]{2,1,0:T(8,128)(2,1)} %get-tuple-element.5.grad_in), custom_call_target="tpu_custom_call" | custom-call | tf_op jit(solution)/shard_map/deliver/pallas_call | solution.py:648

commit v6 on v4

--- a/solution.py
+++ b/solution.py
@@ -336,33 +336,37 @@
             term = value.astype(F32) * (states[:, rows].astype(F32) * gains[:, rows])
             rterm[...] += term[:, :128] + term[:, 128:]
 
+    quarters = [pl.ds(n * 64, 64) for n in range(4)]
+
     def rs_copy(n, part, far, into, send, recv):
-        src, dst, y = [
-            (part.at[y_far, top], far.at[0], y_r),
-            (part.at[y_far, bottom], far.at[1], y_l),
-            (part.at[y_r, bottom], into.at[0, bottom], y_r),
-            (part.at[y_r, top], into.at[0, top], y_r),
-            (part.at[y_l, top], into.at[1, top], y_l),
-            (part.at[y_l, bottom], into.at[1, bottom], y_l),
-        ][n]
+        src, dst, y = (
+            [(part.at[y_far, r], far.at[r], y_r) for r in quarters[:2]]
+            + [(part.at[y_far, r], far.at[r], y_l) for r in quarters[2:]]
+            + [(part.at[y_r, bottom], into.at[0, bottom], y_r)]
+            + [(part.at[y_l, top], into.at[1, top], y_l)]
+            + [(part.at[y_r, r], into.at[0, r], y_r) for r in quarters[:2]]
+            + [(part.at[y_l, r], into.at[1, r], y_l) for r in quarters[2:]]
+        )[n]
         return remote(src, dst, send.at[n], recv.at[n], at_y(y))
 
     def rs_recv(n, part, far, into, send, recv):
-        dst = [
-            far.at[0], far.at[1], into.at[0, bottom], into.at[0, top],
-            into.at[1, top], into.at[1, bottom],
-        ][n]
+        dst = (
+            [far.at[r] for r in quarters]
+            + [into.at[0, bottom], into.at[1, top]]
+            + [into.at[0, r] for r in quarters[:2]]
+            + [into.at[1, r] for r in quarters[2:]]
+        )[n]
         remote(dst, dst, send.at[n], recv.at[n], at_y(y_r)).wait_recv()
 
     def rs_begin(columns, with_rows, args):
         part = args[0]
         piece(columns, y_far, part)
-        rs_copy(0, *args).start()
-        rs_copy(1, *args).start()
+        for n in (0, 2, 1, 3):
+            rs_copy(n, *args).start()
         piece(columns, y_r, part)
-        rs_copy(2, *args).start()
+        rs_copy(4, *args).start()
         piece(columns, y_l, part)
-        rs_copy(4, *args).start()
+        rs_copy(5, *args).start()
         piece(columns, mp, part)
         if with_rows:
             for y in (y_far, y_r, y_l, mp):
@@ -370,15 +374,14 @@
 
     def rs_middle(args):
         part, far = args[:2]
-        rs_recv(0, *args)
-        part[y_r, top] = (part[y_r, top].astype(F32) + far[0].astype(F32)).astype(BF16)
-        rs_copy(3, *args).start()
-        rs_recv(1, *args)
-        part[y_l, bottom] = (part[y_l, bottom].astype(F32) + far[1].astype(F32)).astype(BF16)
-        rs_copy(5, *args).start()
+        for n, y in ((0, y_r), (2, y_l), (1, y_r), (3, y_l)):
+            rs_recv(n, *args)
+            rows = quarters[n]
+            part[y, rows] = (part[y, rows].astype(F32) + far[rows].astype(F32)).astype(BF16)
+            rs_copy(6 + n, *args).start()
 
     def rs_wait(args):
-        for n in (2, 4, 3, 5):
+        for n in range(4, 10):
             rs_recv(n, *args)
 
     l_args = (lpart, lfar, lin, l_s, l_r)
@@ -553,6 +556,7 @@
         layer_out.wait()
         for n in range(6):
             cot_copy(n).wait_send()
+        for n in range(10):
             rs_copy(n, *l_args).wait_send()
         for k in range(1, 8):
             q_copy(lax.rem(me + k, 8)).wait_send()
@@ -570,7 +574,7 @@
         @pl.when(me != i)
         def _():
             g_copy(i).wait_send()
-    for n in range(6):
+    for n in range(10):
         rs_copy(n, *g_args).wait_send()
     for n, y in enumerate((y_r, y_l, y_far)):
         rt_copy(n, y).wait_send()
@@ -623,10 +627,10 @@
             vmem((8, ROWS, 128), BF16),
             vmem((ROWS, 2 * GROUP), BF16),
             vmem((4, ROWS, SLICE), BF16),
-            vmem((2, HALF, SLICE), BF16),
+            vmem((ROWS, SLICE), BF16),
             vmem((2, ROWS, SLICE), BF16),
             vmem((4, ROWS, SLICE), BF16),
-            vmem((2, HALF, SLICE), BF16),
+            vmem((ROWS, SLICE), BF16),
             vmem((2, ROWS, SLICE), BF16),
             vmem((ROWS, 128), F32),
             vmem((8, ROWS), F32),
@@ -636,7 +640,7 @@
             dma(3), dma(4), dma(4), dma(2),
             dma(6), dma(6), dma(8), dma(7), dma(8), dma(4), dma(8), dma(4), dma(3), dma(3),
             dma(4), dma(8), dma(4), dma(8), dma(3), dma(3), dma(4), dma(8),
-            dma(6), dma(6), dma(6), dma(6), dma(3), dma(3),
+            dma(10), dma(10), dma(10), dma(10), dma(3), dma(3),
         ],
         compiler_params=pltpu.CompilerParams(
             collective_id=0, has_side_effects=True, vmem_limit_bytes=56 * 1024 * 1024

time: 74.1 us -> 74.2 us (level)
  no operation moved by 1% of the time
where the time goes in v6:
time: 74.2 us; the launch traced here: 74.1 us
  Pallas kernels  73.5 us (99%)
    pallas_call x1, Pallas kernels, per_device(): pl.pallas_call(kernel, name='window_attention', out_shape=(shape, shape),...  71.4 us
    pallas_call x1, Pallas kernels, per_device(): pl.pallas_call(deliver, name='deliver', out_shape=(shape, shape), grid=(2...  2.04 us

profile of v6, /device:TPU:2, one launch (start us, length us, event | category | flops | bytes accessed | tf_op | source)
XLA Modules:
  0.0 74.1 jit_solution(10195378310171782178)
XLA Ops:
  0.6 71.4 %window_attention.1 = (bf16[1,256,1024]{2,1,0:T(8,128)(2,1)}, bf16[1,256,1024]{2,1,0:T(8,128)(2,1)}) custom-call(s32[1,2]{1,0:T(1,128)} %bitcast.1, bf16[1,256,4096]{2,1,0:T(8,128)(2,1)} %x_hbm.1, f32[1,4096]{1,0:T(1,128)} %gain_hbm.1, bf16[1,4096,2,512]{3,2,1,0:T(2,128)(2,1)} %w_hbm.1, bf16[256,1024]{1,0:T(8,128)(2,1)} %cot_hbm.1), custom_call_target="tpu_custom_call" | custom-call | flops 10000000000 | bytes 12582912 | tf_op jit(solution)/shard_map/window_attention/pallas_call | solution.py:595
  72.1 2.0 %deliver.1 = (bf16[1,256,1024]{2,1,0:T(8,128)(2,1)}, bf16[1,256,1024]{2,1,0:T(8,128)(2,1)}) custom-call(bf16[1,256,1024]{2,1,0:T(8,128)(2,1)} %get-tuple-element.4.seg_in, bf16[1,256,1024]{2,1,0:T(8,128)(2,1)} %get-tuple-element.5.grad_in), custom_call_target="tpu_custom_call" | custom-call | tf_op jit(solution)/shard_map/deliver/pallas_call | solution.py:650
